TPU v7x, 128 devices: a whole 4x4x4 slice. The times are simulated.
128 devices in a mesh: dp: 32 (over y, z_hi, x), seq: 4 (over z_lo, core).
Axes of the slice: x: 4, y: 4, z: 4 (z_hi: 2, z_lo: 2; z = z_hi * 2 + z_lo), core: 2. Of those that a mesh axis runs over, the one named last changes fastest.
Arguments:
- normed: bfloat16 [32768, 7168], P(('dp', 'seq')), may hold values from -24 to 24
- queries: bfloat16 [32768, 3584], P(('dp', 'seq')), may hold values from -32 to 32
- output_gradient: bfloat16 [32768, 3584], P(('dp', 'seq')), may hold values from -6 to 6
- doc_lengths: int32 [32, 8], P('dp'), may hold values from 1 to 512, 1024 in all within a row
- master: float32 [7168, 1024], P('dp'), may hold values from -0.0625 to 0.0625
- moment_one: bfloat16 [7168, 1024], P('dp'), may hold values from -2 to 2
- moment_two: bfloat16 [7168, 1024], P('dp'), may hold values from 0.0009994507 to 0.099609375
Outputs:
- d_queries: bfloat16 [32768, 3584], P(('dp', 'seq'))
- d_normed: bfloat16 [32768, 7168], P(('dp', 'seq'))
- new_master: float32 [7168, 1024], P('dp')
- new_moment_one: bfloat16 [7168, 1024], P('dp')
- new_moment_two: bfloat16 [7168, 1024], P('dp')
All inputs are finite; a program needn't handle non-finite values.
Results may differ from a plain program's by a relative error of at most 0.039.
The roundings to bfloat16 on the way count: a program that leaves them out, or rounds other values in their place, can miss the bound.
Values may be sent and summed in bfloat16 or wider, within the bound.
A program may use at most 192 MiB of HBM per device.

v0:
```python
import jax
import jax.numpy as jnp
from jax import lax
from jax.sharding import PartitionSpec as P

HEAD_SIZE = 128


def on_device(normed, queries, output_gradient, doc_lengths, master, moment_one, moment_two):
    seq_size = lax.axis_size("seq")
    data_size = lax.axis_size("dp")
    tok_rows = normed.shape[0]
    q_width = queries.shape[1]
    kv_width = master.shape[1]
    w_full = lax.all_gather(master.astype(jnp.bfloat16), "dp", axis=0, tiled=True)
    kv_local = jnp.dot(normed, w_full, preferred_element_type=jnp.float32).astype(jnp.bfloat16)
    heads_q, heads_do = (
        lax.all_to_all(
            queries.reshape(tok_rows, seq_size, q_width // seq_size),
            "seq",
            split_axis=1,
            concat_axis=0,
            tiled=True,
        ),
        lax.all_to_all(
            output_gradient.reshape(tok_rows, seq_size, q_width // seq_size),
            "seq",
            split_axis=1,
            concat_axis=0,
            tiled=True,
        ),
    )
    kv_heads = lax.all_to_all(
        kv_local.reshape(tok_rows, seq_size, kv_width // seq_size),
        "seq",
        split_axis=1,
        concat_axis=0,
        tiled=True,
    )
    seq_len = tok_rows * seq_size
    kv_local_heads = kv_width // seq_size // (2 * HEAD_SIZE)
    query_groups = q_width // seq_size // HEAD_SIZE // kv_local_heads
    q_four = heads_q.reshape(seq_len, kv_local_heads, query_groups, HEAD_SIZE)
    do_four = heads_do.reshape(seq_len, kv_local_heads, query_groups, HEAD_SIZE)
    kv_four = kv_heads.reshape(seq_len, kv_local_heads, 2, HEAD_SIZE)
    keys = kv_four[:, :, 0, :]
    values = kv_four[:, :, 1, :]
    doc_ends = jnp.cumsum(doc_lengths[0])
    positions = jnp.arange(seq_len, dtype=jnp.int32)
    doc_ids = jnp.sum((positions[:, None] >= doc_ends[None, :]).astype(jnp.int32), axis=1)
    score_scale = HEAD_SIZE ** (-0.5)
    block_rows = min(512, seq_len)

    def block_step(running, block_index):
        dk_acc, dv_acc = running
        start_row = block_index * block_rows
        q_block = lax.dynamic_slice_in_dim(q_four, start_row, block_rows, 0)
        do_block = lax.dynamic_slice_in_dim(do_four, start_row, block_rows, 0)
        doc_block = lax.dynamic_slice_in_dim(doc_ids, start_row, block_rows, 0)
        pos_block = start_row + jnp.arange(block_rows, dtype=jnp.int32)
        allowed = (doc_block[:, None] == doc_ids[None, :]) & (
            pos_block[:, None] >= positions[None, :]
        )
        scores = (
            jnp.einsum("qhgd,khd->hgqk", q_block, keys, preferred_element_type=jnp.float32)
            * score_scale
        )
        scores = jnp.where(allowed, scores, -1e30)
        row_top = jnp.max(scores, axis=-1, keepdims=True)
        raw = jnp.where(allowed, jnp.exp(scores - row_top), 0.0)
        probability = raw / jnp.sum(raw, axis=-1, keepdims=True)
        prob_half = probability.astype(jnp.bfloat16)
        attended = jnp.einsum(
            "hgqk,khd->qhgd", prob_half, values, preferred_element_type=jnp.float32
        )
        row_delta = jnp.transpose(
            jnp.sum(do_block.astype(jnp.float32) * attended, axis=-1), (1, 2, 0)
        )
        dv_acc = dv_acc + jnp.einsum(
            "hgqk,qhgd->khd", prob_half, do_block, preferred_element_type=jnp.float32
        )
        d_probs = jnp.einsum("qhgd,khd->hgqk", do_block, values, preferred_element_type=jnp.float32)
        d_scores = (probability * (d_probs - row_delta[..., None])).astype(jnp.bfloat16)
        dq_block = (
            jnp.einsum("hgqk,khd->qhgd", d_scores, keys, preferred_element_type=jnp.float32)
            * score_scale
        ).astype(jnp.bfloat16)
        dk_acc = dk_acc + jnp.einsum(
            "hgqk,qhgd->khd", d_scores, q_block, preferred_element_type=jnp.float32
        )
        return ((dk_acc, dv_acc), dq_block)

    empty = jnp.zeros((seq_len, kv_local_heads, HEAD_SIZE), jnp.float32)
    (dk_acc, dv_acc), dq_blocks = lax.scan(
        block_step, (empty, empty), jnp.arange(seq_len // block_rows)
    )
    dq_local = dq_blocks.reshape(seq_len, 1, q_width // seq_size)
    dkv_local = (
        jnp.stack([dk_acc * score_scale, dv_acc], axis=2)
        .astype(jnp.bfloat16)
        .reshape(seq_len, 1, kv_width // seq_size)
    )
    dq_back, dkv_back = (
        lax.all_to_all(dq_local, "seq", split_axis=0, concat_axis=1, tiled=True),
        lax.all_to_all(dkv_local, "seq", split_axis=0, concat_axis=1, tiled=True),
    )
    d_queries = dq_back.reshape(tok_rows, q_width)
    dkv_tok = dkv_back.reshape(tok_rows, kv_width)
    d_normed = lax.dot_general(
        dkv_tok, w_full, (((1,), (1,)), ((), ())), preferred_element_type=jnp.float32
    ).astype(jnp.bfloat16)
    partial_sum = lax.psum_scatter(
        lax.dot_general(
            normed, dkv_tok, (((0,), (0,)), ((), ())), preferred_element_type=jnp.float32
        ).astype(jnp.bfloat16),
        "dp",
        scatter_dimension=0,
        tiled=True,
    )
    grad_total = lax.psum(partial_sum, "seq").astype(jnp.float32)
    grad = grad_total * float(tok_rows * data_size * seq_size) ** (-0.5)
    first = 0.9 * moment_one.astype(jnp.float32) + 0.1 * grad
    second = 0.999 * moment_two.astype(jnp.float32) + 0.001 * grad * grad
    new_master = master - 0.001 * (first / (1.0 - 0.9**3)) / (
        jnp.sqrt(second / (1.0 - 0.999**3)) + 1e-08
    )
    return (
        d_queries,
        d_normed,
        new_master,
        first.astype(jnp.bfloat16),
        second.astype(jnp.bfloat16),
    )


def solution(mesh):
    in_specs = (
        P(("dp", "seq"), None),
        P(("dp", "seq"), None),
        P(("dp", "seq"), None),
        P("dp", None),
        P("dp", None),
        P("dp", None),
        P("dp", None),
    )
    out_specs = (
        P(("dp", "seq"), None),
        P(("dp", "seq"), None),
        P("dp", None),
        P("dp", None),
        P("dp", None),
    )
    return jax.shard_map(
        on_device, mesh=mesh, in_specs=in_specs, out_specs=out_specs, check_vma=False
    )
```

profile of v0, /device:TPU:1, one launch (start us, length us, event | category | flops | bytes accessed | tf_op | source)
XLA Modules:
  0.0 603.4 jit_solution(11297437349422994211)
XLA Ops:
  7.2 2.0 convert_element_type.68
  9.3 3.8 copy.131
  13.1 5.0 all-to-all-start
  18.0 3.8 copy.134
  21.8 21.6 %all-to-all-done = bf16[256,4,896]{0,2,1:T(8,128)(2,1)S(1)} async-done(((bf16[256,4,896]{0,2,1:T(8,128)(2,1)}), bf16[256,4,896]{0,2,1:T(8,128)(2,1)S(1)}, u32[]{:S(2)}, u32[]{:S(2)}) %all-to-all-start) | async-done | bytes 1835040 | tf_op jit(solution)/shard_map/all_to_all | solution.py:18
  43.4 5.1 all-to-all-start.2
  48.6 124.8 %all-gather.2.cloned.1.call-done = bf16[7168,1024]{1,0:T(8,128)(2,1)} async-done(((bf16[224,1024]{1,0:T(8,128)(2,1)}), bf16[7168,1024]{1,0:T(8,128)(2,1)}) %all-gather.2.cloned.1.call-update) | async-done | bytes 14680080 | tf_op jit(solution)/shard_map/all_gather | solution.py:15
  173.4 10.2 %convolution_convert_fusion.1 = bf16[256,1024]{1,0:T(8,128)(2,1)S(1)} fusion(bf16[256,7168]{1,0:T(8,128)(2,1)} %param.9, bf16[7168,1024]{1,0:T(8,128)(2,1)} %all-gather.2.cloned.1.call-done), kind=kOutput, calls=%fused_computation.52 | convolution fusion | flops 3758358528 | bytes 18874368 | tf_op jit(solution)/shard_map/dot_general | solution.py:16
  184.4 4.5 all-to-all-start.1
  189.2 2.6 copy.132
  191.9 3.4 reshape.148
  195.3 4.1 copy.135
  199.4 4.3 reshape.154
  207.3 80.9 %while.15 = (s32[]{:T(128)}, f32[1024,1,128]{0,2,1:T(8,128)S(1)}, f32[1024,1,128]{0,2,1:T(8,128)}, bf16[2,512,1,7,128]{4,1,3,2,0:T(8,128)(2,1)}, s32[2]{0:T(128)...) while((s32[]{:T(128)}, f32[1024,1,128]{0,2,1:T(8,128)S(1)}, ...), condition=%wide.region_6.7_spmd.clone, body=%wide.region_2.6_spmd.clone.sunk | while | flops 5744285696 | bytes 222743072 | solution.py:94
  209.4 2.9 fusion.101
  212.4 4.7 fusion.102
  217.0 5.8 fusion.103
  222.9 7.8 %fusion.104 = bf16[1,7,512,1024]{3,2,1,0:T(8,128)(2,1)} fusion(f32[7,512]{1,0:T(8,128)S(1)} %bitcast.248, f32[7,512]{1,0:T(8,128)S(1)} %fusion.102, f32[7,512]{1,0:T(8,128)S(1)} %get-tuple-element.290, f32[512,7,1024]{2,0,1:T(8,128)S(1)} %get-tuple-element.289, pred[512,1024]{1,0:T(8,128)(4,1)S(1)} %fusion.100, ...), kind=kOutput, calls=%fused_computation.3.clone.1 | convolution fusion | flops 968884224 | bytes 23773188 | tf_op jit(solution)/shard_map/while/body/eval_jaxpr/qhgd,khd->hgqk/dot_general | solution.py:82
  230.7 4.5 fusion.105
  235.2 8.8 %fusion.106 = f32[1024,1,128]{0,2,1:T(8,128)S(1)} fusion(bf16[1024,1,7,128]{0,3,2,1:T(8,128)(2,1)S(1)} %copy-done.3, s32[]{:T(128)S(6)} %select_n.68, f32[1024,1,128]{0,2,1:T(8,128)S(1)} %copy-done.6, pred[]{:T(512)S(6)} %compare.3, f32[7,512]{1,0:T(8,128)S(1)} %fusion.102, f32[7,512]{1,0:T(8,128)S(1)} %get-tuple-element.290, ...), kind=kOutput, calls=%fused_computation.28.clone.1 | convolution fusion | flops 961806336 | bytes 17203204 | tf_op jit(solution)/shard_map/while/body/eval_jaxpr/hgqk,qhgd->khd/dot_general | solution.py:79
  244.0 2.5 fusion.107
  249.6 3.0 fusion.101
  252.6 4.7 fusion.102
  257.3 5.8 fusion.103
  263.1 7.8 %fusion.104 = bf16[1,7,512,1024]{3,2,1,0:T(8,128)(2,1)} fusion(f32[7,512]{1,0:T(8,128)S(1)} %bitcast.248, f32[7,512]{1,0:T(8,128)S(1)} %fusion.102, f32[7,512]{1,0:T(8,128)S(1)} %get-tuple-element.290, f32[512,7,1024]{2,0,1:T(8,128)S(1)} %get-tuple-element.289, pred[512,1024]{1,0:T(8,128)(4,1)S(1)} %fusion.100, ...), kind=kOutput, calls=%fused_computation.3.clone.1 | convolution fusion | flops 968884224 | bytes 23773188 | tf_op jit(solution)/shard_map/while/body/eval_jaxpr/qhgd,khd->hgqk/dot_general | solution.py:82
  271.0 4.5 fusion.105
  275.5 8.8 %fusion.106 = f32[1024,1,128]{0,2,1:T(8,128)S(1)} fusion(bf16[1024,1,7,128]{0,3,2,1:T(8,128)(2,1)S(1)} %copy-done.3, s32[]{:T(128)S(6)} %select_n.68, f32[1024,1,128]{0,2,1:T(8,128)S(1)} %copy-done.6, pred[]{:T(512)S(6)} %compare.3, f32[7,512]{1,0:T(8,128)S(1)} %fusion.102, f32[7,512]{1,0:T(8,128)S(1)} %get-tuple-element.290, ...), kind=kOutput, calls=%fused_computation.28.clone.1 | convolution fusion | flops 961806336 | bytes 17203204 | tf_op jit(solution)/shard_map/while/body/eval_jaxpr/hgqk,qhgd->khd/dot_general | solution.py:79
  284.3 2.5 fusion.107
  291.3 10.9 %all_to_all.75 = bf16[4,2,32768]{2,1,0:T(2,128)(2,1)S(1)} all-to-all(bf16[4,2,32768]{2,1,0:T(2,128)(2,1)S(1)} %reshape.174), channel_id=1, replica_groups=mesh['dp'=32,'seq'=4] {'seq'}, dimensions={0} | all-to-all | bytes 1048576 | tf_op jit(solution)/shard_map/all_to_all | solution.py:105
  303.0 9.4 %convert_bitcast_fusion = bf16[7168,1024]{0,1:T(8,128)(2,1)} fusion(bf16[256,1024]{0,1:T(8,128)(2,1)S(1)} %bitcast.239, bf16[256,7168]{1,0:T(8,128)(2,1)} %param.9), kind=kOutput, calls=%fused_computation.47 | convolution fusion | flops 3765436416 | bytes 18874368 | tf_op jit(solution)/shard_map/dot_general | solution.py:113
  312.4 19.9 %copy.158 = bf16[7168,1024]{1,0:T(8,128)(2,1)} copy(bf16[7168,1024]{0,1:T(8,128)(2,1)} %convert_bitcast_fusion) | data formatting | bytes 29360128
  332.3 2.7 copy.154
  335.1 6.2 %reshape.169 = bf16[1024,1,896]{2,1,0:T(2,128)(2,1)} reshape(bf16[2,512,1,7,128]{4,3,1,0,2:T(8,128)(2,1)S(1)} %copy.154) | data formatting | bytes 3670016 | tf_op jit(solution)/shard_map/reshape | solution.py:97
  341.2 12.1 %reduce.3 = bf16[1024,896]{1,0:T(8,128)(2,1)S(1)} reduce(bf16[1024,1,896]{2,1,0:T(2,128)(2,1)} %reshape.169, bf16[]{:T(256)} %broadcast.64), dimensions={1}, to_apply=%reshape.169.reduce_sub_computation | reduce | bytes 3670018 | tf_op jit(solution)/shard_map/reshape | solution.py:97
  353.3 1.9 reshape.172
  355.3 4.6 all-to-all-start.3
  361.4 2.0 copy.144
  363.4 2.0 copy.143
  365.5 163.3 %reduce-scatter.4.cloned.1.call-done = bf16[224,1024]{1,0:T(8,128)(2,1)} async-done(((bf16[7168,1024]{1,0:T(8,128)(2,1)}), bf16[224,1024]{1,0:T(8,128)(2,1)}) %reduce-scatter.4.cloned.1.call-update) | async-done | bytes 458768
  528.8 2.0 copy.159
  530.8 16.6 %convolution_convert_fusion = bf16[256,7168]{1,0:T(8,128)(2,1)} fusion(bf16[256,1024]{0,1:T(8,128)(2,1)S(1)} %bitcast.240, bf16[7168,1024]{1,0:T(8,128)(2,1)} %all-gather.2.cloned.1.call-done), kind=kOutput, calls=%fused_computation.48 | convolution fusion | flops 3759931392 | bytes 18874368 | tf_op jit(solution)/shard_map/dot_general | solution.py:109
  547.4 3.1 reshape.173
  550.5 3.6 copy.163
  554.1 2.7 copy.140
  556.8 2.6 copy.146
  559.4 29.8 %all-reduce.2.cloned.1.call-done = bf16[224,1024]{0,1:T(8,128)(2,1)} async-done(((bf16[224,1024]{0,1:T(8,128)(2,1)}), bf16[224,1024]{0,1:T(8,128)(2,1)}) %all-reduce.2.cloned.1.call-update) | async-done | bytes 458768 | tf_op jit(solution)/shard_map/psum | solution.py:120
  589.3 3.0 fusion.63
  593.5 2.0 copy.148
  (86 shorter events, 17.3 us)
Async XLA Ops:
  7.2 166.2 %all-gather.2.cloned.1.call-start = ((), (), s32[]{:S(2)}) async-start(), calls=%async_computation.6 | async-start | bytes 15138816 | tf_op jit(solution)/shard_map/all_gather | solution.py:15
  13.1 30.4 %all-to-all-start = ((bf16[256,4,896]{0,2,1:T(8,128)(2,1)}), bf16[256,4,896]{0,2,1:T(8,128)(2,1)S(1)}, u32[]{:S(2)}, u32[]{:S(2)}) async-start(bf16[256,4,896]{0,2,1:T(8,128)(2,1)} %bitcast.236), calls=%async_computation | async-start | bytes 3670016 | tf_op jit(solution)/shard_map/all_to_all | solution.py:18
  43.4 141.0 %all-to-all-start.2 = ((bf16[256,4,896]{0,2,1:T(8,128)(2,1)}), bf16[256,4,896]{0,2,1:T(8,128)(2,1)}, u32[]{:S(2)}, u32[]{:S(2)}) async-start(bf16[256,4,896]{0,2,1:T(8,128)(2,1)} %bitcast.235), calls=%async_computation.2 | async-start | bytes 3670016 | tf_op jit(solution)/shard_map/all_to_all | solution.py:25
  48.6 140.4 %copy-start.9 = (s32[1,8]{1,0:T(1,128)S(1)}, s32[1,8]{1,0:T(1,128)}, u32[]{:S(2)}) copy-start(s32[1,8]{1,0:T(1,128)} %param.12) | copy-start | bytes 100
  184.4 19.3 %all-to-all-start.1 = ((bf16[256,4,256]{2,0,1:T(8,128)(2,1)}), bf16[256,4,256]{2,0,1:T(8,128)(2,1)S(1)}, u32[]{:S(2)}, u32[]{:S(2)}) async-start(bf16[256,4,256]{2,0,1:T(8,128)(2,1)} %bitcast.181), calls=%async_computation.1 | async-start | bytes 1048576 | tf_op jit(solution)/shard_map/all_to_all | solution.py:33
  189.0 339.8 %reduce-scatter.4.cloned.1.call-start = ((), (), s32[]{:S(2)}) async-start(), calls=%async_computation.8 | async-start | bytes 15138816
  212.3 10.5 %copy-start = (f32[512,7,1024]{2,0,1:T(8,128)}, f32[512,7,1024]{2,0,1:T(8,128)S(1)}, u32[]{:S(2)}) copy-start(f32[512,7,1024]{2,0,1:T(8,128)S(1)} %get-tuple-element.289) | copy-start | bytes 44040196 | tf_op jit(solution)/shard_map/while
  212.3 4.7 copy-start.2
  212.3 4.7 copy-start.8
  230.7 4.5 copy-start.3
  230.7 4.5 copy-start.6
  230.7 13.3 %slice-start = ((s8[7340032]{0:T(1024)(128)(4,1)}), s8[4194304]{0:T(1024)(128)(4,1)S(1)}, s32[]{:S(2)}) async-start(s8[7340032]{0:T(1024)(128)(4,1)} %bitcast.231), calls=%async_computation.9 | async-start | bytes 8388608 | tf_op jit(solution)/shard_map/while
  235.2 8.8 %slice-start.1 = ((s8[7340032]{0:T(1024)(128)(4,1)}), s8[3145728]{0:T(1024)(128)(4,1)S(1)}, s32[]{:S(2)}) async-start(s8[7340032]{0:T(1024)(128)(4,1)} %bitcast.231), calls=%async_computation.10 | async-start | bytes 6291456 | tf_op jit(solution)/shard_map/while
  235.2 8.8 %copy-start.4 = (bf16[2,512,1,7,128]{4,1,3,2,0:T(8,128)(2,1)S(1)}, bf16[2,512,1,7,128]{4,1,3,2,0:T(8,128)(2,1)}, u32[]{:S(2)}) copy-start(bf16[2,512,1,7,128]{4,1,3,2,0:T(8,128)(2,1)} %get-tuple-element.308) | copy-start | bytes 5505028 | tf_op jit(solution)/shard_map/while
  244.0 2.5 copy-start.7
  246.5 1.2 copy-start.5
  252.6 10.5 %copy-start = (f32[512,7,1024]{2,0,1:T(8,128)}, f32[512,7,1024]{2,0,1:T(8,128)S(1)}, u32[]{:S(2)}) copy-start(f32[512,7,1024]{2,0,1:T(8,128)S(1)} %get-tuple-element.289) | copy-start | bytes 44040196 | tf_op jit(solution)/shard_map/while
  252.6 4.7 copy-start.2
  252.6 4.7 copy-start.8
  271.0 4.5 copy-start.3
  271.0 4.5 copy-start.6
  271.0 13.3 %slice-start = ((s8[7340032]{0:T(1024)(128)(4,1)}), s8[4194304]{0:T(1024)(128)(4,1)S(1)}, s32[]{:S(2)}) async-start(s8[7340032]{0:T(1024)(128)(4,1)} %bitcast.231), calls=%async_computation.9 | async-start | bytes 8388608 | tf_op jit(solution)/shard_map/while
  275.5 8.8 %slice-start.1 = ((s8[7340032]{0:T(1024)(128)(4,1)}), s8[3145728]{0:T(1024)(128)(4,1)S(1)}, s32[]{:S(2)}) async-start(s8[7340032]{0:T(1024)(128)(4,1)} %bitcast.231), calls=%async_computation.10 | async-start | bytes 6291456 | tf_op jit(solution)/shard_map/while
  275.5 8.8 %copy-start.4 = (bf16[2,512,1,7,128]{4,1,3,2,0:T(8,128)(2,1)S(1)}, bf16[2,512,1,7,128]{4,1,3,2,0:T(8,128)(2,1)}, u32[]{:S(2)}) copy-start(bf16[2,512,1,7,128]{4,1,3,2,0:T(8,128)(2,1)} %get-tuple-element.308) | copy-start | bytes 5505028 | tf_op jit(solution)/shard_map/while
  284.2 2.5 copy-start.7
  286.8 1.2 copy-start.5
  355.3 192.2 %all-to-all-start.3 = ((bf16[4,2,114688]{2,1,0:T(2,128)(2,1)}), bf16[4,2,114688]{2,1,0:T(2,128)(2,1)S(1)}, u32[]{:S(2)}, u32[]{:S(2)}) async-start(bf16[4,2,114688]{2,1,0:T(2,128)(2,1)} %reshape.172), calls=%async_computation.3 | async-start | bytes 3670016 | tf_op jit(solution)/shard_map/all_to_all | solution.py:104
  359.9 229.4 %all-reduce.2.cloned.1.call-start = ((), (), s32[]{:S(2)}) async-start(), calls=%async_computation.7 | async-start | bytes 1048576 | tf_op jit(solution)/shard_map/psum | solution.py:120
  550.5 38.8 %copy-start.1 = (bf16[224,1024]{0,1:T(8,128)(2,1)S(1)}, bf16[224,1024]{0,1:T(8,128)(2,1)}, u32[]{:S(2)}) copy-start(bf16[224,1024]{0,1:T(8,128)(2,1)} %copy.144) | copy-start | bytes 1376260
Sparse Core Ops, SparseCore 0:
  11.5 161.7 all-gather.1
  332.5 196.3 reduce-scatter.3
  531.9 57.3 all-reduce.1
where the time goes:
time: 612 us; the launch traced here: 603 us
  waiting for transfers between devices  340 us (56%)
  matrix products  101 us (17%)
  local copies, waits for them, and re-layouts  86.5 us (14%)
  other arithmetic  30 us (5%)
  starting transfers between devices  19.3 us (3%)
  between operations  14.3 us (2%)
  blocking collectives  10.9 us (2%)
    unnamed x4, waiting for transfers between devices  163 us
    all_gather x1, waiting for transfers between devices, on_device(): lax.all_gather(master.astype(jnp.bfloat16), 'dp', axis=0, tiled=True)  125 us
    unnamed x24, local copies, waits for them, and re-layouts  53.4 us
    psum x1, waiting for transfers between devices, on_device(): grad_total = lax.psum(partial_sum, 'seq').astype(jnp.float32)  29.8 us
    all_to_all x1, waiting for transfers between devices, on_device(): lax.all_to_all(queries.reshape(tok_rows, seq_size, q_width // seq_size),...  21.6 us
    dot_general x2, matrix products, block_step(): jnp.einsum('hgqk,qhgd->khd', prob_half, do_block, preferred_element_type=...  17.5 us
    dot_general x1, matrix products, on_device(): lax.dot_general(dkv_tok, w_full, (((1,), (1,)), ((), ())), preferred_elem...  16.6 us
    dot_general x2, matrix products, block_step(): jnp.einsum('qhgd,khd->hgqk', do_block, values, preferred_element_type=jnp...  15.7 us
  transfers between devices with their start and end apart: 7, of which 4 were waited for; matrix products, arithmetic and copies ran while one was open for 15% of the time, Pallas kernels for 0%

commit v1 on v0

v1 whole, which is shorter than its diff:
```python
import functools
import math

import jax
import jax.numpy as jnp
from jax import lax
from jax.experimental import pallas as pl
from jax.experimental.pallas import tpu as pltpu
from jax.sharding import PartitionSpec as P

HEAD = 128
GROUP = 7
X, Y, ZH = 4, 4, 2
TOK = 256
CT = 512
D = 7168
SHARDS = X * Y * ZH
ROWS = D // SHARDS
HR = ROWS // 2
COLS = 512
HC = COLS // 2
QW = 1792
ROW_BLOCK = X * ROWS
N_BLOCKS = Y * ZH
CHUNK = 128
N_CHUNKS = 5
LANES = GROUP * CHUNK
VMEM_LIMIT = 58 * 1024 * 1024
MESH = pl.DeviceIdType.MESH
ANY = pl.BlockSpec(memory_space=pl.ANY)
F32 = jnp.float32
BF16 = jnp.bfloat16


def dot(a, b, dims=((1,), (0,))):
    return lax.dot_general(a, b, (dims, ((), ())), preferred_element_type=F32)


class Place:
    def __init__(self):
        dp = lax.axis_index("dp")
        sq = lax.axis_index("seq")
        self.dp, self.sq = dp, sq
        self.x = lax.rem(dp, X)
        self.zh = lax.rem(lax.div(dp, X), ZH)
        self.y = lax.div(dp, X * ZH)
        self.core = lax.rem(sq, 2)
        self.zl = lax.div(sq, 2)

    def dev(self, x=None, y=None, zh=None, zl=None, core=None):
        x = self.x if x is None else x
        y = self.y if y is None else y
        zh = self.zh if zh is None else zh
        zl = self.zl if zl is None else zl
        core = self.core if core is None else core
        return ((y * ZH + zh) * X + x, zl * 2 + core)

    def along(self, axis, step):
        if axis == "x":
            return self.dev(x=lax.rem(self.x + step + X, X))
        return self.dev(y=lax.rem(self.y + step + Y, Y))

    def cross(self):
        return self.dev(zh=1 - self.zh, zl=1 - self.zl)

    def partner(self):
        return self.dev(zl=1 - self.zl)

    def other_core(self):
        return self.dev(core=1 - self.core)

    def greet(self):
        barrier = pltpu.get_barrier_semaphore()
        near = [self.along(a, s) for a in ("x", "y") for s in (1, -1)]
        near += [self.cross(), self.partner(), self.other_core()]
        for d in near:
            pl.semaphore_signal(barrier, inc=1, device_id=d, device_id_type=MESH)
        pl.semaphore_wait(barrier, len(near))


class Links:
    def __init__(self, send_sem, recv_sem, place):
        self.send_sem, self.recv_sem, self.place = send_sem, recv_sem, place
        self.index = {}
        self.sent = []

    def _copy(self, key, src, dst, dev):
        k = self.index.setdefault(key, len(self.index))
        return pltpu.make_async_remote_copy(
            src_ref=src,
            dst_ref=dst,
            send_sem=self.send_sem.at[k],
            recv_sem=self.recv_sem.at[k],
            device_id=dev,
            device_id_type=MESH,
        )

    def send(self, key, src, dst, dev):
        copy = self._copy(key, src, dst, dev)
        copy.start()
        self.sent.append(copy)

    def recv(self, key, dst):
        self._copy(key, dst, dst, self.place.other_core()).wait_recv()

    def drain(self):
        for copy in self.sent:
            copy.wait_send()


N_GATHER_SEMS = 96
N_LOCAL_SEMS = 24


def gather_kernel(
    normed, queries, out_grad, master,
    w_out, xt_out, q_out, do_out, kv_out,
    w, xs, xt, mas, kv, acc, send_sem, recv_sem, loc_sem,
):
    here = Place()
    links = Links(send_sem, recv_sem, here)
    n_local = [0]

    def local(src, dst):
        copy = pltpu.make_async_copy(src, dst, loc_sem.at[n_local[0]])
        n_local[0] += 1
        copy.start()
        return copy

    core = here.core
    col = pl.multiple_of(core * COLS, COLS)
    far_col = pl.multiple_of((1 - core) * COLS, COLS)
    del far_col
    own_rows = pl.ds(pl.multiple_of(core * TOK, TOK), TOK)
    far_rows = pl.ds(pl.multiple_of((1 - core) * TOK, TOK), TOK)
    get_master = local(master.at[:, pl.ds(col, COLS)], mas)
    own_normed = local(normed, xs.at[own_rows, :])
    own_q = pl.ds(pl.multiple_of(core * QW, QW), QW)
    far_q = pl.ds(pl.multiple_of((1 - core) * QW, QW), QW)
    pending = [
        local(queries.at[:, own_q], q_out.at[own_rows, :]),
        local(out_grad.at[:, own_q], do_out.at[own_rows, :]),
    ]
    here.greet()
    get_master.wait()

    pos = {"x": here.x, "y": here.y}
    size = {"x": X, "y": Y}

    def slot(p, da, db, zr, half=None):
        first, second = ("x", "y") if p == 0 else ("y", "x")
        at = {
            first: lax.rem(pos[first] + da + size[first], size[first]),
            second: lax.rem(pos[second] + db + size[second], size[second]),
        }
        zh = here.zh if zr == 0 else 1 - here.zh
        s = (at["y"] * ZH + zh) * X + at["x"]
        cols = pl.ds(0, COLS) if half is None else pl.ds(half * HC, HC)
        return w.at[s, pl.ds(p * HR, HR), cols]

    axes = (("x", "y"), ("y", "x"))
    own = (here.y * ZH + here.zh) * X + here.x
    w[own] = mas[...].astype(BF16)

    def send(key, ref, dev):
        links.send(key, ref, ref, dev)

    def second_from(p, da, zr):
        b = axes[p][1]
        for step in (1, -1):
            send(("b", p, zr, da, step, 0), slot(p, da, 0, zr), here.along(b, step))

    def start(zr):
        for p in range(2):
            a = axes[p][0]
            for step in (1, -1):
                send(("a", p, zr, step, 0), slot(p, 0, 0, zr), here.along(a, step))
        for p in range(2):
            second_from(p, 0, zr)

    def forward_first(zr):
        for p in range(2):
            a = axes[p][0]
            for step in (1, -1):
                links.recv(("a", p, zr, step, 0), slot(p, -step, 0, zr))
                half = 0 if step == 1 else 1
                send(("a", p, zr, step, 1), slot(p, -step, 0, zr, half), here.along(a, step))
            for step in (1, -1):
                second_from(p, -step, zr)

    def finish_first(zr):
        for p in range(2):
            for step in (1, -1):
                half = 0 if step == 1 else 1
                links.recv(("a", p, zr, step, 1), slot(p, 2, 0, zr, half))
            second_from(p, 2, zr)

    def forward_second(zr):
        for da in (0, -1, 1, 2):
            for p in range(2):
                b = axes[p][1]
                for step in (1, -1):
                    links.recv(("b", p, zr, da, step, 0), slot(p, da, -step, zr))
                    half = 0 if step == 1 else 1
                    send(
                        ("b", p, zr, da, step, 1),
                        slot(p, da, -step, zr, half),
                        here.along(b, step),
                    )

    def finish_second(zr):
        for da in (0, -1, 1, 2):
            for p in range(2):
                for step in (1, -1):
                    half = 0 if step == 1 else 1
                    links.recv(("b", p, zr, da, step, 1), slot(p, da, 2, zr, half))

    def turn(first, last):
        @pl.loop(first, last)
        def _(b):
            at = pl.ds(pl.multiple_of(b * HEAD, HEAD), HEAD)
            xt[at, :] = xs[:, at].T

    start(0)
    for p in range(2):
        send(("z", p), slot(p, 0, 0, 0), here.cross())
    links.send("normed", normed, xs.at[own_rows, :], here.other_core())
    links.send("q", queries.at[:, far_q], q_out.at[own_rows, :], here.other_core())
    links.send("do", out_grad.at[:, far_q], do_out.at[own_rows, :], here.other_core())
    forward_first(0)
    for p in range(2):
        links.recv(("z", p), slot(p, 0, 0, 1))
    start(1)
    finish_first(0)
    own_normed.wait()
    links.recv("normed", xs.at[far_rows, :])
    turn(0, 14)
    forward_first(1)
    turn(14, 28)
    finish_first(1)
    forward_second(0)
    turn(28, 42)
    forward_second(1)
    turn(42, 56)
    pending.append(local(xt, xt_out))
    finish_second(0)
    finish_second(1)
    pending.append(local(w, w_out))

    acc[...] = jnp.zeros_like(acc)

    @pl.loop(0, N_BLOCKS)
    def _(t):
        at = pl.ds(pl.multiple_of(t * ROW_BLOCK, 128), ROW_BLOCK)
        acc[...] += dot(xs[:, at], w[pl.ds(t * X, X)].reshape(ROW_BLOCK, COLS))

    kv[...] = acc[...].astype(BF16)
    links.send("kv", kv, kv_out.at[pl.ds(0, CT), :], here.partner())
    pending.append(local(kv, kv_out.at[pl.ds(CT, CT), :]))
    links.recv("q", q_out.at[far_rows, :])
    links.recv("do", do_out.at[far_rows, :])
    links.recv("kv", kv_out.at[pl.ds(0, CT), :])
    for copy in pending:
        copy.wait()
    links.drain()


def gather(normed, queries, out_grad, master):
    return pl.pallas_call(
        gather_kernel,
        out_shape=(
            jax.ShapeDtypeStruct((SHARDS, ROWS, COLS), BF16),
            jax.ShapeDtypeStruct((D, CT), BF16),
            jax.ShapeDtypeStruct((CT, QW), BF16),
            jax.ShapeDtypeStruct((CT, QW), BF16),
            jax.ShapeDtypeStruct((2 * CT, COLS), BF16),
        ),
        in_specs=[ANY] * 4,
        out_specs=(ANY,) * 5,
        scratch_shapes=[
            pltpu.VMEM((SHARDS, ROWS, COLS), BF16),
            pltpu.VMEM((CT, D), BF16),
            pltpu.VMEM((D, CT), BF16),
            pltpu.VMEM((ROWS, COLS), F32),
            pltpu.VMEM((CT, COLS), BF16),
            pltpu.VMEM((CT, COLS), F32),
            pltpu.SemaphoreType.DMA((N_GATHER_SEMS,)),
            pltpu.SemaphoreType.DMA((N_GATHER_SEMS,)),
            pltpu.SemaphoreType.DMA((N_LOCAL_SEMS,)),
        ],
        compiler_params=pltpu.CompilerParams(
            collective_id=0, has_side_effects=True, vmem_limit_bytes=VMEM_LIMIT
        ),
        name="gather_project",
    )(normed, queries, out_grad, master)


def attention_kernel(
    lengths, q_ref, do_ref, kv_ref, dq_ref, dkv_ref,
    qs, dos, prob, dprob, dq_t, dk_acc, dv_acc,
):
    zl = lax.div(lax.axis_index("seq"), 2)
    first_abs = zl * CT
    scale = HEAD ** (-0.5)
    to_base2 = scale * math.log2(math.e)
    ends = []
    total = lengths[0, 0]
    ends.append(total)
    for j in range(1, lengths.shape[1]):
        total = total + lengths[0, j]
        ends.append(total)
    dk_acc[...] = jnp.zeros_like(dk_acc)
    dv_acc[...] = jnp.zeros_like(dv_acc)
    lane = lax.broadcasted_iota(jnp.int32, (1, LANES), 1)
    lane_tok = lax.rem(lane, CHUNK)
    sub = lax.broadcasted_iota(jnp.int32, (CHUNK, 1), 0)

    @pl.loop(0, CT // CHUNK)
    def _(i):
        q_abs = first_abs + i * CHUNK + lane_tok
        doc_start = jnp.zeros_like(q_abs)
        first_q = first_abs + i * CHUNK
        first_start = jnp.int32(0)
        for e in ends:
            doc_start = jnp.where(q_abs >= e, jnp.maximum(doc_start, e), doc_start)
            first_start = jnp.where(first_q >= e, jnp.maximum(first_start, e), first_start)
        shift = CT - first_abs
        doc_start = doc_start + shift
        q_row = q_abs + shift
        last = CT // CHUNK + i
        lowest = lax.div(first_start + shift, CHUNK)
        lowest = jnp.maximum(lowest, last - (N_CHUNKS - 1))
        rows = pl.ds(pl.multiple_of(i * CHUNK, CHUNK), CHUNK)
        for a in range(GROUP):
            qs[a * CHUNK : (a + 1) * CHUNK, :] = q_ref[rows, a * HEAD : (a + 1) * HEAD]
            dos[a * CHUNK : (a + 1) * CHUNK, :] = do_ref[rows, a * HEAD : (a + 1) * HEAD]
        dq_t[...] = jnp.zeros_like(dq_t)

        def scores(j, top):
            at = pl.ds(pl.multiple_of(j * CHUNK, CHUNK), CHUNK)
            s = dot(kv_ref[at, 0:HEAD], qs[...], ((1,), (1,)))
            k_row = j * CHUNK + sub
            s = jnp.where((k_row >= doc_start) & (k_row <= q_row), s, -1e30)
            prob[j - lowest] = s
            return jnp.maximum(top, jnp.max(s, axis=0, keepdims=True))

        top = lax.fori_loop(lowest, last + 1, scores, jnp.full((1, LANES), -3e38, F32))

        def weigh(j, sums):
            mass, delta = sums
            at = pl.ds(pl.multiple_of(j * CHUNK, CHUNK), CHUNK)
            p = jnp.exp2((prob[j - lowest] - top) * to_base2)
            dp = dot(kv_ref[at, HEAD : 2 * HEAD], dos[...], ((1,), (1,)))
            prob[j - lowest] = p
            dprob[j - lowest] = dp
            mass = mass + jnp.sum(p, axis=0, keepdims=True)
            delta = delta + jnp.sum(p * dp, axis=0, keepdims=True)
            return mass, delta

        zero = jnp.zeros((1, LANES), F32)
        mass, delta = lax.fori_loop(lowest, last + 1, weigh, (zero, zero))
        inv = 1.0 / mass
        delta = delta * inv

        def back(j, carry):
            at = pl.ds(pl.multiple_of(j * CHUNK, CHUNK), CHUNK)
            p = prob[j - lowest] * inv
            ds = (p * (dprob[j - lowest] - delta)).astype(BF16)
            dv_acc[at, :] += dot(p.astype(BF16), dos[...])
            dk_acc[at, :] += dot(ds, qs[...])
            dq_t[...] += dot(kv_ref[at, 0:HEAD], ds, ((0,), (0,)))
            return carry

        lax.fori_loop(lowest, last + 1, back, 0)
        for a in range(GROUP):
            part = dq_t[:, a * CHUNK : (a + 1) * CHUNK].T * scale
            dq_ref[rows, a * HEAD : (a + 1) * HEAD] = part.astype(BF16)

    dkv_ref[:, 0:HEAD] = (dk_acc[...] * scale).astype(BF16)
    dkv_ref[:, HEAD : 2 * HEAD] = dv_acc[...].astype(BF16)


def attention(lengths, q, do, kv):
    heads = COLS // (2 * HEAD)
    width = GROUP * HEAD
    return pl.pallas_call(
        attention_kernel,
        grid=(heads,),
        out_shape=(
            jax.ShapeDtypeStruct((CT, QW), BF16),
            jax.ShapeDtypeStruct((2 * CT, COLS), BF16),
        ),
        in_specs=[
            pl.BlockSpec(memory_space=pltpu.SMEM),
            pl.BlockSpec((CT, width), lambda g: (0, g)),
            pl.BlockSpec((CT, width), lambda g: (0, g)),
            pl.BlockSpec((2 * CT, 2 * HEAD), lambda g: (0, g)),
        ],
        out_specs=(
            pl.BlockSpec((CT, width), lambda g: (0, g)),
            pl.BlockSpec((2 * CT, 2 * HEAD), lambda g: (0, g)),
        ),
        scratch_shapes=[
            pltpu.VMEM((LANES, HEAD), BF16),
            pltpu.VMEM((LANES, HEAD), BF16),
            pltpu.VMEM((N_CHUNKS, CHUNK, LANES), F32),
            pltpu.VMEM((N_CHUNKS, CHUNK, LANES), F32),
            pltpu.VMEM((HEAD, LANES), F32),
            pltpu.VMEM((2 * CT, HEAD), F32),
            pltpu.VMEM((2 * CT, HEAD), F32),
        ],
        compiler_params=pltpu.CompilerParams(vmem_limit_bytes=VMEM_LIMIT),
        name="attention_back",
    )(lengths, q, do, kv)


N_REDUCE_SEMS = 96


def reduce_kernel(
    xt_in, w_in, dkv_in, dq_in, master, moment_one, moment_two,
    dq_out, dn_out, master_out, one_out, two_out,
    xt, w, term, dkv, dkv_far,
    opp_a, low_a, high_a, opp_b, low_b, high_b,
    opp2_a, low2_a, high2_a, opp2_b, low2_b, high2_b,
    z_in, l_in, mine, total, dn_send, dn_recv, dn_own,
    mas, one, two, send_sem, recv_sem, loc_sem,
):
    here = Place()
    links = Links(send_sem, recv_sem, here)
    n_local = [0]

    def local(src, dst):
        copy = pltpu.make_async_copy(src, dst, loc_sem.at[n_local[0]])
        n_local[0] += 1
        copy.start()
        return copy

    core = here.core
    own_rows = pl.ds(pl.multiple_of(core * TOK, TOK), TOK)
    far_rows = pl.ds(pl.multiple_of((1 - core) * TOK, TOK), TOK)
    own_q = pl.ds(pl.multiple_of(core * QW, QW), QW)
    get_dkv = local(dkv_in.at[pl.ds(CT, CT), :], dkv)
    get_xt = local(xt_in, xt)
    here.greet()

    @pl.when(here.zl == 1)
    def _():
        pltpu.make_async_remote_copy(
            src_ref=dkv_in.at[pl.ds(0, CT), :],
            dst_ref=dkv_far,
            send_sem=send_sem.at[N_REDUCE_SEMS - 1],
            recv_sem=recv_sem.at[N_REDUCE_SEMS - 1],
            device_id=here.partner(),
            device_id_type=MESH,
        ).start()

    get_w = local(w_in, w)
    pending = [local(dq_in.at[own_rows, :], dq_out.at[:, own_q])]
    links.send("dq", dq_in.at[far_rows, :], dq_out.at[:, own_q], here.other_core())
    get_master = local(master, mas)
    get_one = local(moment_one, one)
    get_two = local(moment_two, two)
    get_dkv.wait()

    @pl.when(here.zl == 0)
    def _():
        pltpu.make_async_remote_copy(
            src_ref=dkv_far,
            dst_ref=dkv_far,
            send_sem=send_sem.at[N_REDUCE_SEMS - 1],
            recv_sem=recv_sem.at[N_REDUCE_SEMS - 1],
            device_id=here.partner(),
            device_id_type=MESH,
        ).wait_recv()
        dkv[...] = (dkv[...].astype(F32) + dkv_far[...].astype(F32)).astype(BF16)

    get_xt.wait()

    pos = {"x": here.x, "y": here.y}
    size = {"x": X, "y": Y}
    axes = (("x", "y"), ("y", "x"))

    def at_axis(axis, off):
        return lax.rem(pos[axis] + off + size[axis], size[axis])

    class Ring:
        def __init__(self, name, axis, slot, opp, low, high):
            self.name, self.axis, self.slot = name, axis, slot
            self.opp, self.low, self.high = opp, low, high

        def half(self, ref, h):
            return ref.at[:, :, pl.ds(h * HC, HC)]

        def send_far(self):
            for h, step in ((0, 1), (1, -1)):
                links.send(
                    (self.name, "far", step),
                    self.half(self.slot(2), h), self.opp(h), here.along(self.axis, step),
                )

        def send_near(self, step):
            h, land = (1, self.low) if step == 1 else (0, self.high)
            links.send(
                (self.name, "near", step),
                self.half(self.slot(step), h), self.half(land(), h), here.along(self.axis, step),
            )

        def forward(self):
            for h, step in ((0, 1), (1, -1)):
                links.recv((self.name, "far", step), self.opp(h))
                here_sum = self.half(self.slot(step), h)
                here_sum[...] = (
                    here_sum[...].astype(F32) + self.opp(h)[...].astype(F32)
                ).astype(BF16)
                land = self.low if step == 1 else self.high
                links.send(
                    (self.name, "sum", step),
                    here_sum, self.half(land(), h), here.along(self.axis, step),
                )

        def finish(self):
            for h, step in ((1, 1), (0, -1)):
                land = self.low if step == 1 else self.high
                links.recv((self.name, "near", step), self.half(land(), h))
                links.recv((self.name, "sum", step), self.half(land(), 1 - h))
            mine_ref = self.slot(0)
            mine_ref[...] = (
                mine_ref[...].astype(F32)
                + self.low()[...].astype(F32)
                + self.high()[...].astype(F32)
            ).astype(BF16)

    def rows_of(p):
        return pl.ds(p * HR, HR)

    def term_at(y, x, p):
        return term.at[y, :, x, rows_of(p), :]

    def first_ring(p, k, off):
        a, b = axes[p]
        opp, low, high = ((opp_a, low_a, high_a), (opp_b, low_b, high_b))[p]

        def slot(da):
            at = {a: at_axis(a, da), b: at_axis(b, off)}
            return term_at(at["y"], at["x"], p)

        return Ring(("first", p, k), a, slot, lambda h: opp.at[k, h], lambda: low.at[k], lambda: high.at[k])

    def second_ring(p):
        a, b = axes[p]
        opp, low, high = ((opp2_a, low2_a, high2_a), (opp2_b, low2_b, high2_b))[p]

        def slot(db):
            at = {a: pos[a], b: at_axis(b, db)}
            return term_at(at["y"], at["x"], p)

        return Ring(("second", p), b, slot, lambda h: opp.at[h], lambda: low, lambda: high)

    offs = (2, 1, -1, 0)
    rings = [[first_ring(p, k, off) for k, off in enumerate(offs)] for p in range(2)]
    finals = [second_ring(p) for p in range(2)]

    def make_terms(off):
        y = at_axis("y", off)
        for z in range(ZH):
            at = pl.ds(pl.multiple_of((y * ZH + z) * ROW_BLOCK, 128), ROW_BLOCK)
            t = dot(xt[at, :], dkv[...]).astype(BF16)
            term[y, z] = t.reshape(X, ROWS, COLS)

    def dn_far(t):
        at = pl.ds(t * ROW_BLOCK, ROW_BLOCK)
        w_t = w[pl.ds(t * X, X)].reshape(ROW_BLOCK, COLS)
        dn_send[:, at] = dot(dkv[far_rows, :], w_t, ((1,), (1,))).astype(BF16)
        links.send(("dn", t), dn_send.at[:, at], dn_recv.at[:, at], here.other_core())

    def dn_near(t):
        at = pl.ds(t * ROW_BLOCK, ROW_BLOCK)
        w_t = w[pl.ds(t * X, X)].reshape(ROW_BLOCK, COLS)
        near = dot(dkv[own_rows, :], w_t, ((1,), (1,)))
        links.recv(("dn", t), dn_recv.at[:, at])
        dn_own[:, at] = (near + dn_recv[:, at].astype(F32)).astype(BF16)
        pending.append(local(dn_own.at[:, at], dn_out.at[:, at]))

    make_terms(2)
    rings[0][0].send_far()
    for k in range(4):
        rings[1][k].send_far()
    for step in (1, -1):
        rings[0][0].send_near(step)
    make_terms(1)
    rings[0][1].send_far()
    for k in range(4):
        rings[1][k].send_near(1)
    make_terms(-1)
    rings[0][2].send_far()
    for k in range(4):
        rings[1][k].send_near(-1)
    make_terms(0)
    rings[0][3].send_far()
    for k in range(1, 4):
        for step in (1, -1):
            rings[0][k].send_near(step)
    get_w.wait()
    for k in range(4):
        for p in range(2):
            rings[p][k].forward()
        dn_far(2 * k)
        dn_far(2 * k + 1)
    for k in range(4):
        for p in range(2):
            rings[p][k].finish()
            if k == 0:
                finals[p].send_far()
            elif k == 1:
                finals[p].send_near(1)
            elif k == 2:
                finals[p].send_near(-1)
        dn_near(2 * k)
        dn_near(2 * k + 1)
    for p in range(2):
        finals[p].forward()

    own_z = here.zh
    far_z = 1 - here.zh
    for p in range(2):
        finals[p].finish()
        links.send(
            ("z", p),
            term.at[here.y, far_z, here.x, rows_of(p), :], z_in.at[rows_of(p), :], here.cross(),
        )
    for p in range(2):
        rows = rows_of(p)
        links.recv(("z", p), z_in.at[rows, :])
        mine[rows, :] = (
            term[here.y, own_z, here.x, rows, :].astype(F32) + z_in[rows, :].astype(F32)
        ).astype(BF16)
        links.send(("l", p), mine.at[rows, :], l_in.at[rows, :], here.partner())
    for p in range(2):
        rows = rows_of(p)
        links.recv(("l", p), l_in.at[rows, :])
        total[core, rows, :] = mine[rows, :].astype(F32) + l_in[rows, :].astype(F32)
        links.send(
            ("c", p), total.at[core, rows, :], total.at[core, rows, :], here.other_core()
        )
    for p in range(2):
        links.recv(("c", p), total.at[1 - core, rows_of(p), :])
    get_master.wait()
    get_one.wait()
    get_two.wait()
    tokens = TOK * lax.axis_size("dp") * lax.axis_size("seq")
    for h in range(2):
        cols = pl.ds(h * COLS, COLS)
        grad = total[h] * float(tokens) ** (-0.5)
        first = 0.9 * one[:, cols].astype(F32) + 0.1 * grad
        second = 0.999 * two[:, cols].astype(F32) + 0.001 * grad * grad
        mas[:, cols] = mas[:, cols] - 0.001 * (first / (1.0 - 0.9**3)) / (
            jnp.sqrt(second / (1.0 - 0.999**3)) + 1e-08
        )
        one[:, cols] = first.astype(BF16)
        two[:, cols] = second.astype(BF16)
    pending.append(local(mas, master_out))
    pending.append(local(one, one_out))
    pending.append(local(two, two_out))
    links.recv("dq", dq_out.at[:, pl.ds(pl.multiple_of((1 - core) * QW, QW), QW)])
    for copy in pending:
        copy.wait()
    links.drain()

    @pl.when(here.zl == 1)
    def _():
        pltpu.make_async_remote_copy(
            src_ref=dkv_in.at[pl.ds(0, CT), :],
            dst_ref=dkv_far,
            send_sem=send_sem.at[N_REDUCE_SEMS - 1],
            recv_sem=recv_sem.at[N_REDUCE_SEMS - 1],
            device_id=here.partner(),
            device_id_type=MESH,
        ).wait_send()


def reduce_update(xt, w, dkv, dq, master, moment_one, moment_two):
    ring4 = [
        pltpu.VMEM((4, 2, ZH, HR, HC), BF16),
        pltpu.VMEM((4, ZH, HR, COLS), BF16),
        pltpu.VMEM((4, ZH, HR, COLS), BF16),
    ]
    ring1 = [
        pltpu.VMEM((2, ZH, HR, HC), BF16),
        pltpu.VMEM((ZH, HR, COLS), BF16),
        pltpu.VMEM((ZH, HR, COLS), BF16),
    ]
    width = master.shape[1]
    return pl.pallas_call(
        reduce_kernel,
        out_shape=(
            jax.ShapeDtypeStruct((TOK, 2 * QW), BF16),
            jax.ShapeDtypeStruct((TOK, D), BF16),
            jax.ShapeDtypeStruct((ROWS, width), F32),
            jax.ShapeDtypeStruct((ROWS, width), BF16),
            jax.ShapeDtypeStruct((ROWS, width), BF16),
        ),
        in_specs=[ANY] * 7,
        out_specs=(ANY,) * 5,
        scratch_shapes=[
            pltpu.VMEM((D, CT), BF16),
            pltpu.VMEM((SHARDS, ROWS, COLS), BF16),
            pltpu.VMEM((Y, ZH, X, ROWS, COLS), BF16),
            pltpu.VMEM((CT, COLS), BF16),
            pltpu.VMEM((CT, COLS), BF16),
            *ring4, *ring4, *ring1, *ring1,
            pltpu.VMEM((ROWS, COLS), BF16),
            pltpu.VMEM((ROWS, COLS), BF16),
            pltpu.VMEM((ROWS, COLS), BF16),
            pltpu.VMEM((2, ROWS, COLS), F32),
            pltpu.VMEM((TOK, D), BF16),
            pltpu.VMEM((TOK, D), BF16),
            pltpu.VMEM((TOK, D), BF16),
            pltpu.VMEM((ROWS, width), F32),
            pltpu.VMEM((ROWS, width), BF16),
            pltpu.VMEM((ROWS, width), BF16),
            pltpu.SemaphoreType.DMA((N_REDUCE_SEMS,)),
            pltpu.SemaphoreType.DMA((N_REDUCE_SEMS,)),
            pltpu.SemaphoreType.DMA((N_LOCAL_SEMS,)),
        ],
        compiler_params=pltpu.CompilerParams(
            collective_id=1, has_side_effects=True, vmem_limit_bytes=VMEM_LIMIT
        ),
        name="reduce_update",
    )(xt, w, dkv, dq, master, moment_one, moment_two)


def on_device(normed, queries, output_gradient, doc_lengths, master, moment_one, moment_two):
    w, xt, q, do, kv = gather(normed, queries, output_gradient, master)
    dq, dkv = attention(doc_lengths, q, do, kv)
    return reduce_update(xt, w, dkv, dq, master, moment_one, moment_two)


def solution(mesh):
    rows = P(("dp", "seq"), None)
    shard = P("dp", None)
    return jax.shard_map(
        on_device,
        mesh=mesh,
        in_specs=(rows, rows, rows, shard, shard, shard, shard),
        out_specs=(rows, rows, shard, shard, shard),
        check_vma=False,
    )
```

time: 612 us -> 174 us (0.28); the launches traced: 603 us -> 174 us
  waiting for transfers between devices: 340 us -> 0 us
  Pallas kernels: 0 us -> 165 us
  matrix products: 101 us -> 0 us
  local copies, waits for them, and re-layouts: 86.5 us -> 7.68 us
  other arithmetic: 30 us -> 0 us
  starting transfers between devices: 19.3 us -> 0 us
  between operations: 14.3 us -> 0.66 us
  blocking collectives: 10.9 us -> 0 us
    pallas_call x0 -> x3, Pallas kernels: none -> 165 us  [the longest x1 86.9 us: reduce_update(): pl.pallas_call(reduce_kernel, out_shape=(jax.ShapeDtypeStruct((TOK, 2 * Q...]
    unnamed x4 -> x0, waiting for transfers between devices: 163 us -> none
    all_gather x1 -> x0, waiting for transfers between devices: 125 us -> none  [on_device(): lax.all_gather(master.astype(jnp.bfloat16), 'dp', axis=0, tiled=True)]
    dot_general x15 -> x0, matrix products: 101 us -> none  [the longest x2 17.5 us: block_step(): jnp.einsum('hgqk,qhgd->khd', prob_half, do_block, preferred_element_type=...]
    unnamed x24 -> x13, local copies, waits for them, and re-layouts: 53.4 us -> 7.68 us
    psum x1 -> x0, waiting for transfers between devices: 29.8 us -> none  [on_device(): grad_total = lax.psum(partial_sum, 'seq').astype(jnp.float32)]
    all_to_all x4 -> x0, waiting for transfers between devices: 21.6 us -> none  [the longest x1 21.6 us: on_device(): lax.all_to_all(queries.reshape(tok_rows, seq_size, q_width // seq_size),...]
    all_to_all x4 -> x0, starting transfers between devices: 19.2 us -> none  [the longest x1 5.13 us: on_device(): lax.all_to_all(output_gradient.reshape(tok_rows, seq_size, q_width // seq...]
  transfers between devices with their start and end apart: 7 -> 0, of which waited for: 4 -> 0; matrix products, arithmetic and copies ran while one was open for 15% -> 0% of each run, Pallas kernels for 0% -> 0%
where the time goes in v1:
time: 174 us
  Pallas kernels  165 us (95%)
  local copies, waits for them, and re-layouts  7.68 us (4%)
    pallas_call x1, Pallas kernels, reduce_update(): pl.pallas_call(reduce_kernel, out_shape=(jax.ShapeDtypeStruct((TOK, 2 * Q...  86.9 us
    pallas_call x1, Pallas kernels, gather(): pl.pallas_call(gather_kernel, out_shape=(jax.ShapeDtypeStruct((SHARDS, RO...  61.2 us
    pallas_call x1, Pallas kernels, attention(): pl.pallas_call(attention_kernel, grid=(heads,), out_shape=(jax.ShapeDtype...  17.3 us
    unnamed x13, local copies, waits for them, and re-layouts  7.68 us

profile of v1, /device:TPU:1, one launch (start us, length us, event | category | flops | bytes accessed | tf_op | source)
XLA Modules:
  0.0 173.7 jit_solution(5410745777949301886)
XLA Ops:
  0.6 61.2 %gather_project.1 = (bf16[32,224,512]{2,1,0:T(8,128)(2,1)}, bf16[7168,512]{1,0:T(8,128)(2,1)}, bf16[512,1792]{1,0:T(8,128)(2,1)}, bf16[512,1792]{1,0:T(8,128)(2,1)}, bf16[1024,512]{1,0:T(8,128)(2,1)}) custom-call(bf16[256,7168]{1,0:T(8,128)(2,1)} %normed.1, bf16[256,3584]{1,0:T(8,128)(2,1)} %queries.1, bf16[256,3584]{1,0:T(8,128)(2,1)} %out_grad.1, ...), custom_call_target="tpu_custom_call" | custom-call | tf_op jit(solution)/shard_map/gather_project/pallas_call | solution.py:269
  61.8 17.3 %attention_back.1 = (bf16[512,1792]{1,0:T(8,128)(2,1)}, bf16[1024,512]{1,0:T(8,128)(2,1)}) custom-call(s32[1,8]{1,0:T(1,128)} %lengths.1, bf16[512,1792]{1,0:T(8,128)(2,1)} %get-tuple-element.14.q_ref, bf16[512,1792]{1,0:T(8,128)(2,1)} %get-tuple-element.15.do_ref, bf16[1024,512]{1,0:T(8,128)(2,1)} %get-tuple-element.16.kv_ref), custom_call_target="tpu_custom_call" | custom-call | tf_op jit(solution)/shard_map/attention_back/pallas_call | solution.py:386
  79.1 86.9 %reduce_update.1 = (bf16[256,3584]{1,0:T(8,128)(2,1)}, bf16[256,7168]{1,0:T(8,128)(2,1)}, f32[224,1024]{1,0:T(8,128)}, bf16[224,1024]{1,0:T(8,128)(2,1)}, bf16[224,1024]{1,0:T(8,128)(2,1)}) custom-call(bf16[7168,512]{1,0:T(8,128)(2,1)} %get-tuple-element.12.xt_in, bf16[32,224,512]{2,1,0:T(8,128)(2,1)} %get-tuple-element.13.w_in, ...), custom_call_target="tpu_custom_call" | custom-call | tf_op jit(solution)/shard_map/reduce_update/pallas_call | solution.py:694
  166.0 0.0 copy-start
  166.0 3.0 %copy.17 = bf16[256,3584]{1,0:T(8,128)(2,1)} copy(bf16[256,3584]{1,0:T(8,128)(2,1)} %get-tuple-element.24) | data formatting | bytes 3670016
  169.0 0.0 copy-done
  169.0 0.0 copy-start.1
  169.0 1.8 %copy.18 = bf16[256,7168]{1,0:T(8,128)(2,1)} copy(bf16[256,7168]{1,0:T(8,128)(2,1)S(1)} %copy-done) | data formatting | bytes 7340032
  170.8 0.0 copy-done.1
  170.8 0.0 copy-start.3
  170.8 0.0 copy-start.2
  170.8 0.9 copy.19
  171.8 0.4 copy-done.3
  172.1 0.8 copy.20
  172.9 0.0 copy-done.2
  172.9 0.8 copy.21
Async XLA Ops:
  166.0 3.0 %copy-start = (bf16[256,7168]{1,0:T(8,128)(2,1)S(1)}, bf16[256,7168]{1,0:T(8,128)(2,1)}, u32[]{:S(2)}) copy-start(bf16[256,7168]{1,0:T(8,128)(2,1)} %get-tuple-element.25) | copy-start | bytes 11010052
  169.0 1.8 %copy-start.1 = (f32[224,1024]{1,0:T(8,128)S(1)}, f32[224,1024]{1,0:T(8,128)}, u32[]{:S(2)}) copy-start(f32[224,1024]{1,0:T(8,128)} %get-tuple-element.26) | copy-start | bytes 2752516
  170.8 1.3 copy-start.3
  170.8 2.1 %copy-start.2 = (bf16[224,1024]{1,0:T(8,128)(2,1)S(1)}, bf16[224,1024]{1,0:T(8,128)(2,1)}, u32[]{:S(2)}) copy-start(bf16[224,1024]{1,0:T(8,128)(2,1)} %get-tuple-element.28) | copy-start | bytes 1376260

commit v2 on v1

v2 whole, which is shorter than its diff:
```python
import functools
import math

import jax
import jax.numpy as jnp
from jax import lax
from jax.experimental import pallas as pl
from jax.experimental.pallas import tpu as pltpu
from jax.sharding import PartitionSpec as P

HEAD = 128
GROUP = 7
X, Y, ZH = 4, 4, 2
TOK = 256
CT = 512
D = 7168
SHARDS = X * Y * ZH
ROWS = D // SHARDS
PARTS = (
    (0, 80, ("x", "y"), True),
    (80, 64, ("y", "x"), True),
    (144, 32, ("x", "y"), False),
    (176, 48, ("y", "x"), False),
)
Z_FIRST = (0, 1)
Z_LAST = (2, 3)
SEQ = 1024
COLS = 512
HC = COLS // 2
QW = 896
ROW_BLOCK = X * ROWS
N_BLOCKS = Y * ZH
CHUNK = 128
N_CHUNKS = 5
LANES = GROUP * CHUNK
VMEM_LIMIT = 58 * 1024 * 1024
MESH = pl.DeviceIdType.MESH
ANY = pl.BlockSpec(memory_space=pl.ANY)
F32 = jnp.float32
BF16 = jnp.bfloat16


def dot(a, b, dims=((1,), (0,))):
    return lax.dot_general(a, b, (dims, ((), ())), preferred_element_type=F32)


class Place:
    def __init__(self):
        dp = lax.axis_index("dp")
        sq = lax.axis_index("seq")
        self.dp, self.sq = dp, sq
        self.x = lax.rem(dp, X)
        self.zh = lax.rem(lax.div(dp, X), ZH)
        self.y = lax.div(dp, X * ZH)
        self.core = lax.rem(sq, 2)
        self.zl = lax.div(sq, 2)

    def dev(self, x=None, y=None, zh=None, zl=None, core=None):
        x = self.x if x is None else x
        y = self.y if y is None else y
        zh = self.zh if zh is None else zh
        zl = self.zl if zl is None else zl
        core = self.core if core is None else core
        return ((y * ZH + zh) * X + x, zl * 2 + core)

    def along(self, axis, step):
        if axis == "x":
            return self.dev(x=lax.rem(self.x + step + X, X))
        return self.dev(y=lax.rem(self.y + step + Y, Y))

    def cross(self):
        return self.dev(zh=1 - self.zh, zl=1 - self.zl)

    def partner(self):
        return self.dev(zl=1 - self.zl)

    def other_core(self):
        return self.dev(core=1 - self.core)

    def greet(self):
        barrier = pltpu.get_barrier_semaphore()
        near = [self.along(a, s) for a in ("x", "y") for s in (1, -1)]
        near += [self.cross(), self.partner(), self.other_core()]
        near.append(self.dev(zl=1 - self.zl, core=1 - self.core))
        for d in near:
            pl.semaphore_signal(barrier, inc=1, device_id=d, device_id_type=MESH)
        pl.semaphore_wait(barrier, len(near))


class Links:
    def __init__(self, send_sem, recv_sem, place):
        self.send_sem, self.recv_sem, self.place = send_sem, recv_sem, place
        self.index = {}
        self.sent = []

    def _copy(self, key, src, dst, dev):
        k = self.index.setdefault(key, len(self.index))
        return pltpu.make_async_remote_copy(
            src_ref=src,
            dst_ref=dst,
            send_sem=self.send_sem.at[k],
            recv_sem=self.recv_sem.at[k],
            device_id=dev,
            device_id_type=MESH,
        )

    def send(self, key, src, dst, dev):
        copy = self._copy(key, src, dst, dev)
        copy.start()
        self.sent.append(copy)

    def recv(self, key, dst):
        self._copy(key, dst, dst, self.place.other_core()).wait_recv()

    def drain(self):
        for copy in self.sent:
            copy.wait_send()


N_GATHER_SEMS = 176
N_LOCAL_SEMS = 40


def gather_kernel(
    normed, queries, out_grad, master,
    w_out, xt_out, q_out, do_out, kv_out,
    w, xs, xt, mas, kv, acc, q_src, do_src, q_all, do_all, send_sem, recv_sem, loc_sem,
):
    here = Place()
    links = Links(send_sem, recv_sem, here)
    n_local = [0]

    def local(src, dst):
        copy = pltpu.make_async_copy(src, dst, loc_sem.at[n_local[0]])
        n_local[0] += 1
        copy.start()
        return copy

    core, zl = here.core, here.zl
    own_rows = pl.ds(pl.multiple_of(core * TOK, TOK), TOK)
    far_rows = pl.ds(pl.multiple_of((1 - core) * TOK, TOK), TOK)

    def seq_rows(sq):
        return pl.ds(pl.multiple_of(sq * TOK, TOK), TOK)

    def head_cols(zl_to, core_to):
        return pl.ds(pl.multiple_of((core_to * 2 + zl_to) * QW, 128), QW)

    get_master = local(master.at[:, pl.ds(pl.multiple_of(core * COLS, COLS), COLS)], mas)
    get_q = local(queries, q_src)
    get_do = local(out_grad, do_src)
    own_normed = local(normed, xs.at[own_rows, :])
    own_q = local(queries.at[:, head_cols(zl, core)], q_all.at[seq_rows(here.sq), :])
    own_do = local(out_grad.at[:, head_cols(zl, core)], do_all.at[seq_rows(here.sq), :])
    pending = []
    here.greet()
    get_master.wait()

    pos = {"x": here.x, "y": here.y}
    size = {"x": X, "y": Y}

    def at_axis(axis, off):
        return lax.rem(pos[axis] + off + size[axis], size[axis])

    def slot(p, da, db, zr, half=None):
        row, rows, axes, _ = PARTS[p]
        at = {axes[0]: at_axis(axes[0], da), axes[1]: at_axis(axes[1], db)}
        zh = here.zh if zr == 0 else 1 - here.zh
        s = (at["y"] * ZH + zh) * X + at["x"]
        cols = pl.ds(0, COLS) if half is None else pl.ds(half * HC, HC)
        return w.at[s, pl.ds(row, rows), cols]

    own = (here.y * ZH + here.zh) * X + here.x
    w[own] = mas[...].astype(BF16)

    def send(key, ref, dev):
        links.send(key, ref, ref, dev)

    def second_from(p, da, zr):
        b = PARTS[p][2][1]
        for step in (1, -1):
            send(("b", p, zr, da, step, 0), slot(p, da, 0, zr), here.along(b, step))

    def start(parts, zr):
        for p in parts:
            a = PARTS[p][2][0]
            for step in (1, -1):
                send(("a", p, zr, step, 0), slot(p, 0, 0, zr), here.along(a, step))
        for p in parts:
            second_from(p, 0, zr)

    def over_z(p, da, db):
        if p in Z_LAST:
            send(("z", p, da, db), slot(p, da, db, 0), here.cross())

    def forward_first(parts, zr):
        for p in parts:
            a = PARTS[p][2][0]
            for step in (1, -1):
                links.recv(("a", p, zr, step, 0), slot(p, -step, 0, zr))
                half = 0 if step == 1 else 1
                send(("a", p, zr, step, 1), slot(p, -step, 0, zr, half), here.along(a, step))
            for step in (1, -1):
                second_from(p, -step, zr)
                over_z(p, -step, 0)

    def finish_first(parts, zr):
        for p in parts:
            for step in (1, -1):
                half = 0 if step == 1 else 1
                links.recv(("a", p, zr, step, 1), slot(p, 2, 0, zr, half))
            second_from(p, 2, zr)
            over_z(p, 2, 0)

    def forward_second(parts, zr):
        for da in (0, -1, 1, 2):
            for p in parts:
                b = PARTS[p][2][1]
                for step in (1, -1):
                    links.recv(("b", p, zr, da, step, 0), slot(p, da, -step, zr))
                    half = 0 if step == 1 else 1
                    send(
                        ("b", p, zr, da, step, 1),
                        slot(p, da, -step, zr, half),
                        here.along(b, step),
                    )
                    over_z(p, da, -step)

    def finish_second(parts, zr):
        for da in (0, -1, 1, 2):
            for p in parts:
                for step in (1, -1):
                    half = 0 if step == 1 else 1
                    links.recv(("b", p, zr, da, step, 1), slot(p, da, 2, zr, half))
                over_z(p, da, 2)

    def turn(first, last):
        @pl.loop(first, last)
        def _(b):
            at = pl.ds(pl.multiple_of(b * HEAD, HEAD), HEAD)
            xt[at, :] = xs[:, at].T

    start(Z_LAST, 0)
    start(Z_FIRST, 0)
    for p in Z_FIRST:
        send(("z", p), slot(p, 0, 0, 0), here.cross())
    for p in Z_LAST:
        over_z(p, 0, 0)
    links.send("normed", normed, xs.at[own_rows, :], here.other_core())
    get_q.wait()
    get_do.wait()
    others = (("p", 1 - zl, core), ("c", zl, 1 - core), ("d", 1 - zl, 1 - core))
    for name, src, dst in (("q", q_src, q_all), ("do", do_src, do_all)):
        for way, zl_to, core_to in others:
            links.send(
                (name, way),
                src.at[:, head_cols(zl_to, core_to)], dst.at[seq_rows(here.sq), :],
                here.dev(zl=zl_to, core=core_to),
            )
    forward_first(Z_LAST, 0)
    forward_first(Z_FIRST, 0)
    finish_first(Z_LAST, 0)
    for p in Z_FIRST:
        links.recv(("z", p), slot(p, 0, 0, 1))
    start(Z_FIRST, 1)
    finish_first(Z_FIRST, 0)
    own_normed.wait()
    links.recv("normed", xs.at[far_rows, :])
    turn(0, 14)
    forward_second(Z_LAST, 0)
    forward_first(Z_FIRST, 1)
    turn(14, 28)
    finish_second(Z_LAST, 0)
    finish_first(Z_FIRST, 1)
    turn(28, 42)
    forward_second(Z_FIRST, 0)
    turn(42, 56)
    pending.append(local(xt, xt_out))
    forward_second(Z_FIRST, 1)
    finish_second(Z_FIRST, 0)
    finish_second(Z_FIRST, 1)
    for p in Z_LAST:
        for da in (0, -1, 1, 2):
            for db in (0, -1, 1, 2):
                links.recv(("z", p, da, db), slot(p, da, db, 1))
    pending.append(local(w, w_out))

    own_tokens = pl.ds(pl.multiple_of(zl * CT, CT), CT)
    for far in (True, False):
        head = 1 - zl if far else zl
        cols = pl.ds(pl.multiple_of(head * HC, HC), HC)
        acc[...] = jnp.zeros_like(acc)

        @pl.loop(0, N_BLOCKS)
        def _(t):
            at = pl.ds(pl.multiple_of(t * ROW_BLOCK, 128), ROW_BLOCK)
            w_t = w[pl.ds(t * X, X), :, cols].reshape(ROW_BLOCK, HC)
            acc[...] += dot(xs[:, at], w_t)

        if far:
            kv[0] = acc[...].astype(BF16)
            links.send("kv", kv.at[0], kv_out.at[own_tokens, :], here.partner())
        else:
            kv[1] = acc[...].astype(BF16)
            pending.append(local(kv.at[1], kv_out.at[own_tokens, :]))
    own_q.wait()
    own_do.wait()
    for name, dst in (("q", q_all), ("do", do_all)):
        for way, zl_to, core_to in others:
            links.recv((name, way), dst.at[seq_rows(zl_to * 2 + core_to), :])
    pending.append(local(q_all, q_out))
    pending.append(local(do_all, do_out))
    links.recv("kv", kv_out.at[pl.ds(pl.multiple_of((1 - zl) * CT, CT), CT), :])
    for copy in pending:
        copy.wait()
    links.drain()


def gather(normed, queries, out_grad, master):
    return pl.pallas_call(
        gather_kernel,
        out_shape=(
            jax.ShapeDtypeStruct((SHARDS, ROWS, COLS), BF16),
            jax.ShapeDtypeStruct((D, CT), BF16),
            jax.ShapeDtypeStruct((SEQ, QW), BF16),
            jax.ShapeDtypeStruct((SEQ, QW), BF16),
            jax.ShapeDtypeStruct((SEQ, HC), BF16),
        ),
        in_specs=[ANY] * 4,
        out_specs=(ANY,) * 5,
        scratch_shapes=[
            pltpu.VMEM((SHARDS, ROWS, COLS), BF16),
            pltpu.VMEM((CT, D), BF16),
            pltpu.VMEM((D, CT), BF16),
            pltpu.VMEM((ROWS, COLS), F32),
            pltpu.VMEM((2, CT, HC), BF16),
            pltpu.VMEM((CT, HC), F32),
            pltpu.VMEM(queries.shape, BF16),
            pltpu.VMEM(queries.shape, BF16),
            pltpu.VMEM((SEQ, QW), BF16),
            pltpu.VMEM((SEQ, QW), BF16),
            pltpu.SemaphoreType.DMA((N_GATHER_SEMS,)),
            pltpu.SemaphoreType.DMA((N_GATHER_SEMS,)),
            pltpu.SemaphoreType.DMA((N_LOCAL_SEMS,)),
        ],
        compiler_params=pltpu.CompilerParams(
            collective_id=0, has_side_effects=True, vmem_limit_bytes=VMEM_LIMIT
        ),
        name="gather_project",
    )(normed, queries, out_grad, master)


def attention_kernel(
    lengths, q_ref, do_ref, kv_ref, dq_ref, dkv_ref,
    qs, dos, prob, dprob, dq_t, dk_acc, dv_acc,
):
    i = pl.program_id(0)
    scale = HEAD ** (-0.5)
    to_base2 = scale * math.log2(math.e)
    ends = []
    total = lengths[0, 0]
    ends.append(total)
    for j in range(1, lengths.shape[1]):
        total = total + lengths[0, j]
        ends.append(total)

    @pl.when(i == 0)
    def _():
        dk_acc[...] = jnp.zeros_like(dk_acc)
        dv_acc[...] = jnp.zeros_like(dv_acc)

    lane = lax.broadcasted_iota(jnp.int32, (1, LANES), 1)
    sub = lax.broadcasted_iota(jnp.int32, (CHUNK, 1), 0)
    q_row = i * CHUNK + lax.rem(lane, CHUNK)
    doc_start = jnp.zeros_like(q_row)
    first_start = jnp.int32(0)
    for e in ends:
        doc_start = jnp.where(q_row >= e, jnp.maximum(doc_start, e), doc_start)
        first_start = jnp.where(i * CHUNK >= e, jnp.maximum(first_start, e), first_start)
    lowest = lax.div(first_start, CHUNK)
    lowest = jnp.maximum(lowest, i - (N_CHUNKS - 1))
    for a in range(GROUP):
        qs[a * CHUNK : (a + 1) * CHUNK, :] = q_ref[:, a * HEAD : (a + 1) * HEAD]
        dos[a * CHUNK : (a + 1) * CHUNK, :] = do_ref[:, a * HEAD : (a + 1) * HEAD]
    dq_t[...] = jnp.zeros_like(dq_t)

    def scores(j, top):
        at = pl.ds(pl.multiple_of(j * CHUNK, CHUNK), CHUNK)
        s = dot(kv_ref[at, 0:HEAD], qs[...], ((1,), (1,)))
        k_row = j * CHUNK + sub
        s = jnp.where((k_row >= doc_start) & (k_row <= q_row), s, -1e30)
        prob[j - lowest] = s
        return jnp.maximum(top, jnp.max(s, axis=0, keepdims=True))

    top = lax.fori_loop(lowest, i + 1, scores, jnp.full((1, LANES), -3e38, F32))

    def weigh(j, sums):
        mass, delta = sums
        at = pl.ds(pl.multiple_of(j * CHUNK, CHUNK), CHUNK)
        p = jnp.exp2((prob[j - lowest] - top) * to_base2)
        dp = dot(kv_ref[at, HEAD : 2 * HEAD], dos[...], ((1,), (1,)))
        prob[j - lowest] = p
        dprob[j - lowest] = dp
        mass = mass + jnp.sum(p, axis=0, keepdims=True)
        delta = delta + jnp.sum(p * dp, axis=0, keepdims=True)
        return mass, delta

    zero = jnp.zeros((1, LANES), F32)
    mass, delta = lax.fori_loop(lowest, i + 1, weigh, (zero, zero))
    inv = 1.0 / mass
    delta = delta * inv

    def back(j, carry):
        at = pl.ds(pl.multiple_of(j * CHUNK, CHUNK), CHUNK)
        p = prob[j - lowest] * inv
        ds = (p * (dprob[j - lowest] - delta)).astype(BF16)
        dv_acc[at, :] += dot(p.astype(BF16), dos[...])
        dk_acc[at, :] += dot(ds, qs[...])
        dq_t[...] += dot(kv_ref[at, 0:HEAD], ds, ((0,), (0,)))
        return carry

    lax.fori_loop(lowest, i + 1, back, 0)
    for a in range(GROUP):
        part = dq_t[:, a * CHUNK : (a + 1) * CHUNK].T * scale
        dq_ref[:, a * HEAD : (a + 1) * HEAD] = part.astype(BF16)

    @pl.when(i == pl.num_programs(0) - 1)
    def _():
        dkv_ref[:, 0:HEAD] = (dk_acc[...] * scale).astype(BF16)
        dkv_ref[:, HEAD : 2 * HEAD] = dv_acc[...].astype(BF16)


def attention(lengths, q, do, kv):
    return pl.pallas_call(
        attention_kernel,
        grid=(SEQ // CHUNK,),
        out_shape=(
            jax.ShapeDtypeStruct((SEQ, QW), BF16),
            jax.ShapeDtypeStruct((SEQ, HC), BF16),
        ),
        in_specs=[
            pl.BlockSpec(memory_space=pltpu.SMEM),
            pl.BlockSpec((CHUNK, QW), lambda i: (i, 0)),
            pl.BlockSpec((CHUNK, QW), lambda i: (i, 0)),
            pl.BlockSpec((SEQ, HC), lambda i: (0, 0)),
        ],
        out_specs=(
            pl.BlockSpec((CHUNK, QW), lambda i: (i, 0)),
            pl.BlockSpec((SEQ, HC), lambda i: (0, 0)),
        ),
        scratch_shapes=[
            pltpu.VMEM((LANES, HEAD), BF16),
            pltpu.VMEM((LANES, HEAD), BF16),
            pltpu.VMEM((N_CHUNKS, CHUNK, LANES), F32),
            pltpu.VMEM((N_CHUNKS, CHUNK, LANES), F32),
            pltpu.VMEM((HEAD, LANES), F32),
            pltpu.VMEM((SEQ, HEAD), F32),
            pltpu.VMEM((SEQ, HEAD), F32),
        ],
        compiler_params=pltpu.CompilerParams(vmem_limit_bytes=VMEM_LIMIT),
        name="attention_back",
    )(lengths, q, do, kv)


N_REDUCE_SEMS = 176


def reduce_kernel(
    xt_in, w_in, dkv_in, dq_in,
    dq_out, dn_out, grad_out,
    xt, w, term, dkv, dq_src, dq_all, z_early, z_in, l_in, mine, total, dn_send, dn_recv, dn_own,
    *rest,
):
    bufs = [rest[6 * p : 6 * p + 6] for p in range(4)]
    send_sem, recv_sem, loc_sem = rest[24:]
    here = Place()
    links = Links(send_sem, recv_sem, here)
    n_local = [0]

    def local(src, dst):
        copy = pltpu.make_async_copy(src, dst, loc_sem.at[n_local[0]])
        n_local[0] += 1
        copy.start()
        return copy

    core, zl = here.core, here.zl
    own_z, far_z = here.zh, 1 - here.zh
    own_rows = pl.ds(pl.multiple_of(core * TOK, TOK), TOK)
    far_rows = pl.ds(pl.multiple_of((1 - core) * TOK, TOK), TOK)
    own_tokens = pl.ds(pl.multiple_of(zl * CT, CT), CT)
    far_tokens = pl.ds(pl.multiple_of((1 - zl) * CT, CT), CT)

    def seq_rows(sq):
        return pl.ds(pl.multiple_of(sq * TOK, TOK), TOK)

    def head_cols(zl_of, core_of):
        return pl.ds(pl.multiple_of((core_of * 2 + zl_of) * QW, 128), QW)

    get_dkv = local(dkv_in.at[own_tokens, :], dkv.at[zl])
    get_xt = local(xt_in, xt)
    get_dq = local(dq_in, dq_src)
    own_dq = local(dq_in.at[seq_rows(here.sq), :], dq_all.at[:, head_cols(zl, core)])
    here.greet()
    links.send("dkv", dkv_in.at[far_tokens, :], dkv.at[zl], here.partner())
    get_w = local(w_in, w)
    pending = []
    get_dkv.wait()
    get_xt.wait()
    links.recv("dkv", dkv.at[1 - zl])

    pos = {"x": here.x, "y": here.y}
    size = {"x": X, "y": Y}

    def at_axis(axis, off):
        return lax.rem(pos[axis] + off + size[axis], size[axis])

    class Ring:
        def __init__(self, name, axis, slot, opp, low, high):
            self.name, self.axis, self.slot = name, axis, slot
            self.opp, self.low, self.high = opp, low, high

        def half(self, ref, h):
            return ref.at[:, :, pl.ds(h * HC, HC)]

        def send_far(self):
            for h, step in ((0, 1), (1, -1)):
                links.send(
                    (self.name, "far", step),
                    self.half(self.slot(2), h), self.opp(h), here.along(self.axis, step),
                )

        def send_near(self, step):
            h, land = (1, self.low) if step == 1 else (0, self.high)
            links.send(
                (self.name, "near", step),
                self.half(self.slot(step), h), self.half(land(), h), here.along(self.axis, step),
            )

        def forward(self):
            for h, step in ((0, 1), (1, -1)):
                links.recv((self.name, "far", step), self.opp(h))
                here_sum = self.half(self.slot(step), h)
                here_sum[...] = (
                    here_sum[...].astype(F32) + self.opp(h)[...].astype(F32)
                ).astype(BF16)
                land = self.low if step == 1 else self.high
                links.send(
                    (self.name, "sum", step),
                    here_sum, self.half(land(), h), here.along(self.axis, step),
                )

        def finish(self):
            for h, step in ((1, 1), (0, -1)):
                land = self.low if step == 1 else self.high
                links.recv((self.name, "near", step), self.half(land(), h))
                links.recv((self.name, "sum", step), self.half(land(), 1 - h))
            mine_ref = self.slot(0)
            mine_ref[...] = (
                mine_ref[...].astype(F32)
                + self.low()[...].astype(F32)
                + self.high()[...].astype(F32)
            ).astype(BF16)

    def rows_of(p):
        return pl.ds(PARTS[p][0], PARTS[p][1])

    def term_at(at, p):
        zs = pl.ds(0, ZH) if p in Z_FIRST else pl.ds(own_z, 1)
        return term.at[at["y"], zs, at["x"], rows_of(p), :]

    def first_ring(p, k, off):
        a, b = PARTS[p][2]
        opp, low, high = bufs[p][:3]

        def slot(da):
            return term_at({a: at_axis(a, da), b: at_axis(b, off)}, p)

        return Ring(
            ("first", p, k), a, slot,
            lambda h: opp.at[k, h], lambda: low.at[k], lambda: high.at[k],
        )

    def second_ring(p):
        a, b = PARTS[p][2]
        opp, low, high = bufs[p][3:]

        def slot(db):
            return term_at({a: pos[a], b: at_axis(b, db)}, p)

        return Ring(("second", p), b, slot, lambda h: opp.at[h], lambda: low, lambda: high)

    offs = (2, 1, -1, 0)
    rings = [[first_ring(p, k, off) for k, off in enumerate(offs)] for p in range(4)]
    finals = [second_ring(p) for p in range(4)]
    late = pl.ds(PARTS[2][0], PARTS[2][1] + PARTS[3][1])

    def make_terms(k):
        y = at_axis("y", offs[k])
        for z in (far_z, own_z):
            at = pl.ds(pl.multiple_of((y * ZH + z) * ROW_BLOCK, 128), ROW_BLOCK)
            for h in range(2):
                t = dot(xt[at, :], dkv[h]).astype(BF16)
                term[y, z, :, :, h * HC : (h + 1) * HC] = t.reshape(X, ROWS, HC)
        links.send(
            ("early", k), term.at[y, far_z, :, late, :], z_early.at[k], here.cross()
        )

    def add_early(k):
        y = at_axis("y", offs[k])
        links.recv(("early", k), z_early.at[k])
        into = term.at[y, own_z, :, late, :]
        into[...] = (into[...].astype(F32) + z_early[k].astype(F32)).astype(BF16)

    def launch(k, p_x, p_y):
        rings[p_x][k].send_far()
        for step in (1, -1):
            rings[p_x][k].send_near(step)
        for piece in rings[p_y]:
            if k == 0:
                piece.send_far()
            elif k < 3:
                piece.send_near(offs[k])

    def dn_far(t):
        at = pl.ds(t * ROW_BLOCK, ROW_BLOCK)
        partial = jnp.zeros((TOK, ROW_BLOCK), F32)
        for h in range(2):
            w_t = w[pl.ds(t * X, X), :, h * HC : (h + 1) * HC].reshape(ROW_BLOCK, HC)
            partial += dot(dkv[h, far_rows, :], w_t, ((1,), (1,)))
        dn_send[:, at] = partial.astype(BF16)
        links.send(("dn", t), dn_send.at[:, at], dn_recv.at[:, at], here.other_core())

    def dn_near(t):
        at = pl.ds(t * ROW_BLOCK, ROW_BLOCK)
        links.recv(("dn", t), dn_recv.at[:, at])
        partial = dn_recv[:, at].astype(F32)
        for h in range(2):
            w_t = w[pl.ds(t * X, X), :, h * HC : (h + 1) * HC].reshape(ROW_BLOCK, HC)
            partial += dot(dkv[h, own_rows, :], w_t, ((1,), (1,)))
        dn_own[:, at] = partial.astype(BF16)
        pending.append(local(dn_own.at[:, at], dn_out.at[:, at]))

    for k in range(4):
        make_terms(k)
        launch(k, 0, 1)
    get_dq.wait()
    others = (("p", 1 - zl, core), ("c", zl, 1 - core), ("d", 1 - zl, 1 - core))
    for way, zl_to, core_to in others:
        links.send(
            ("dq", way),
            dq_src.at[seq_rows(zl_to * 2 + core_to), :], dq_all.at[:, head_cols(zl, core)],
            here.dev(zl=zl_to, core=core_to),
        )
    get_w.wait()
    for k in range(4):
        for p in Z_FIRST:
            rings[p][k].forward()
        add_early(k)
        launch(k, 2, 3)
        dn_far(2 * k)
        dn_far(2 * k + 1)

    def end_first(k, parts):
        for p in parts:
            rings[p][k].finish()
            if k == 0:
                finals[p].send_far()
            elif k < 3:
                finals[p].send_near(offs[k])

    for k in range(4):
        for p in Z_LAST:
            rings[p][k].forward()
        end_first(k, Z_FIRST)
        dn_near(2 * k)
        dn_near(2 * k + 1)
    for p in Z_FIRST:
        finals[p].forward()
    for k in range(4):
        end_first(k, Z_LAST)
    for p in Z_FIRST:
        finals[p].finish()
        rows = rows_of(p)
        links.send(
            ("z", p), term.at[here.y, far_z, here.x, rows, :], z_in.at[rows, :], here.cross()
        )
    for p in Z_LAST:
        finals[p].forward()

    def to_partner(p):
        rows = rows_of(p)
        links.send(("l", p), mine.at[rows, :], l_in.at[rows, :], here.partner())

    for p in Z_FIRST:
        rows = rows_of(p)
        links.recv(("z", p), z_in.at[rows, :])
        mine[rows, :] = (
            term[here.y, own_z, here.x, rows, :].astype(F32) + z_in[rows, :].astype(F32)
        ).astype(BF16)
        to_partner(p)
    for p in Z_LAST:
        finals[p].finish()
        rows = rows_of(p)
        mine[rows, :] = term[here.y, own_z, here.x, rows, :]
        to_partner(p)
    for p in range(4):
        rows = rows_of(p)
        links.recv(("l", p), l_in.at[rows, :])
        total[core, rows, :] = mine[rows, :].astype(F32) + l_in[rows, :].astype(F32)
        links.send(
            ("c", p), total.at[core, rows, :], total.at[core, rows, :], here.other_core()
        )
    own_dq.wait()
    for way, zl_to, core_to in others:
        links.recv(("dq", way), dq_all.at[:, head_cols(zl_to, core_to)])
    pending.append(local(dq_all, dq_out))
    for p in range(4):
        links.recv(("c", p), total.at[1 - core, rows_of(p), :])
    pending.append(local(total, grad_out))
    for copy in pending:
        copy.wait()
    links.drain()


def reduce_terms(xt, w, dkv, dq):
    rings = []
    for p, (_, rows, _, both) in enumerate(PARTS):
        nz = ZH if both else 1
        rings += [
            pltpu.VMEM((4, 2, nz, rows, HC), BF16),
            pltpu.VMEM((4, nz, rows, COLS), BF16),
            pltpu.VMEM((4, nz, rows, COLS), BF16),
            pltpu.VMEM((2, nz, rows, HC), BF16),
            pltpu.VMEM((nz, rows, COLS), BF16),
            pltpu.VMEM((nz, rows, COLS), BF16),
        ]
    late = PARTS[2][1] + PARTS[3][1]
    return pl.pallas_call(
        reduce_kernel,
        out_shape=(
            jax.ShapeDtypeStruct((TOK, 4 * QW), BF16),
            jax.ShapeDtypeStruct((TOK, D), BF16),
            jax.ShapeDtypeStruct((2, ROWS, COLS), F32),
        ),
        in_specs=[ANY] * 4,
        out_specs=(ANY,) * 3,
        scratch_shapes=[
            pltpu.VMEM((D, CT), BF16),
            pltpu.VMEM((SHARDS, ROWS, COLS), BF16),
            pltpu.VMEM((Y, ZH, X, ROWS, COLS), BF16),
            pltpu.VMEM((2, CT, HC), BF16),
            pltpu.VMEM((SEQ, QW), BF16),
            pltpu.VMEM((TOK, 4 * QW), BF16),
            pltpu.VMEM((4, X, late, COLS), BF16),
            pltpu.VMEM((ROWS, COLS), BF16),
            pltpu.VMEM((ROWS, COLS), BF16),
            pltpu.VMEM((ROWS, COLS), BF16),
            pltpu.VMEM((2, ROWS, COLS), F32),
            pltpu.VMEM((TOK, D), BF16),
            pltpu.VMEM((TOK, D), BF16),
            pltpu.VMEM((TOK, D), BF16),
            *rings,
            pltpu.SemaphoreType.DMA((N_REDUCE_SEMS,)),
            pltpu.SemaphoreType.DMA((N_REDUCE_SEMS,)),
            pltpu.SemaphoreType.DMA((N_LOCAL_SEMS,)),
        ],
        compiler_params=pltpu.CompilerParams(
            collective_id=1, has_side_effects=True, vmem_limit_bytes=VMEM_LIMIT
        ),
        name="reduce_terms",
    )(xt, w, dkv, dq)


STEPS = 7


def update_kernel(
    tokens, dq_in, dn_in, total, master, moment_one, moment_two,
    dq_out, dn_out, master_out, one_out, two_out,
):
    dq_out[...] = dq_in[...]
    dn_out[...] = dn_in[...]
    for h in range(2):
        cols = pl.ds(h * COLS, COLS)
        grad = total[h] * float(tokens) ** (-0.5)
        first = 0.9 * moment_one[:, cols].astype(F32) + 0.1 * grad
        second = 0.999 * moment_two[:, cols].astype(F32) + 0.001 * grad * grad
        master_out[:, cols] = master[:, cols] - 0.001 * (first / (1.0 - 0.9**3)) / (
            jnp.sqrt(second / (1.0 - 0.999**3)) + 1e-08
        )
        one_out[:, cols] = first.astype(BF16)
        two_out[:, cols] = second.astype(BF16)


def update(tokens, dq, dn, total, master, moment_one, moment_two):
    def across(a):
        return pl.BlockSpec((a.shape[0], a.shape[1] // STEPS), lambda i: (0, i))

    def down(a):
        return pl.BlockSpec((a.shape[0] // STEPS, a.shape[1]), lambda i: (i, 0))

    return pl.pallas_call(
        functools.partial(update_kernel, tokens),
        grid=(STEPS,),
        out_shape=tuple(
            jax.ShapeDtypeStruct(a.shape, a.dtype) for a in (dq, dn, master, moment_one, moment_two)
        ),
        in_specs=[
            across(dq),
            across(dn),
            pl.BlockSpec((2, ROWS // STEPS, COLS), lambda i: (0, i, 0)),
            down(master),
            down(moment_one),
            down(moment_two),
        ],
        out_specs=(across(dq), across(dn), down(master), down(moment_one), down(moment_two)),
        compiler_params=pltpu.CompilerParams(vmem_limit_bytes=VMEM_LIMIT),
        name="update",
    )(dq, dn, total, master, moment_one, moment_two)


def on_device(normed, queries, output_gradient, doc_lengths, master, moment_one, moment_two):
    w, xt, q, do, kv = gather(normed, queries, output_gradient, master)
    dq, dkv = attention(doc_lengths, q, do, kv)
    dq, dn, total = reduce_terms(xt, w, dkv, dq)
    tokens = normed.shape[0] * lax.axis_size("dp") * lax.axis_size("seq")
    return update(tokens, dq, dn, total, master, moment_one, moment_two)


def solution(mesh):
    rows = P(("dp", "seq"), None)
    shard = P("dp", None)
    return jax.shard_map(
        on_device,
        mesh=mesh,
        in_specs=(rows, rows, rows, shard, shard, shard, shard),
        out_specs=(rows, rows, shard, shard, shard),
        check_vma=False,
    )
```

time: 174 us -> 154 us (0.89)
  Pallas kernels: 165 us -> 152 us
  local copies, waits for them, and re-layouts: 7.68 us -> 0 us
    unnamed x13 -> x0, local copies, waits for them, and re-layouts: 7.68 us -> none
    pallas_call x1, Pallas kernels: 61.2 us -> 54.5 us  [gather(): pl.pallas_call(gather_kernel, out_shape=(jax.ShapeDtypeStruct((SHARDS, RO...]
    pallas_call x2 -> x3, Pallas kernels: 104 us -> 97.9 us  [the longest x1 70.1 us: reduce_terms(): pl.pallas_call(reduce_kernel, out_shape=(jax.ShapeDtypeStruct((TOK, 4 * Q...]
where the time goes in v2:
time: 154 us; the launch traced here: 153 us
  Pallas kernels  152 us (99%)
    pallas_call x1, Pallas kernels, reduce_terms(): pl.pallas_call(reduce_kernel, out_shape=(jax.ShapeDtypeStruct((TOK, 4 * Q...  70.1 us
    pallas_call x1, Pallas kernels, gather(): pl.pallas_call(gather_kernel, out_shape=(jax.ShapeDtypeStruct((SHARDS, RO...  54.5 us
    pallas_call x1, Pallas kernels, attention(): pl.pallas_call(attention_kernel, grid=(SEQ // CHUNK,), out_shape=(jax.Sha...  19.3 us
    pallas_call x1, Pallas kernels, update(): pl.pallas_call(functools.partial(update_kernel, tokens), grid=(STEPS,), o...  8.53 us

profile of v2, /device:TPU:1, one launch (start us, length us, event | category | flops | bytes accessed | tf_op | source)
XLA Modules:
  0.0 153.3 jit_solution(12357825509140734280)
XLA Ops:
  0.6 54.5 %gather_project.1 = (bf16[32,224,512]{2,1,0:T(8,128)(2,1)}, bf16[7168,512]{1,0:T(8,128)(2,1)}, bf16[1024,896]{1,0:T(8,128)(2,1)}, bf16[1024,896]{1,0:T(8,128)(2,1)}, bf16[1024,256]{1,0:T(8,128)(2,1)}) custom-call(bf16[256,7168]{1,0:T(8,128)(2,1)} %normed.1, bf16[256,3584]{1,0:T(8,128)(2,1)} %queries.1, bf16[256,3584]{1,0:T(8,128)(2,1)} %out_grad.1, ...), custom_call_target="tpu_custom_call" | custom-call | tf_op jit(solution)/shard_map/gather_project/pallas_call | solution.py:320
  55.2 19.3 %attention_back.1 = (bf16[1024,896]{1,0:T(8,128)(2,1)}, bf16[1024,256]{1,0:T(8,128)(2,1)}) custom-call(s32[1,8]{1,0:T(1,128)} %lengths.1, bf16[1024,896]{1,0:T(8,128)(2,1)} %get-tuple-element.17.q_ref, bf16[1024,896]{1,0:T(8,128)(2,1)} %get-tuple-element.18.do_ref, bf16[1024,256]{1,0:T(8,128)(2,1)} %get-tuple-element.19.kv_ref), custom_call_target="tpu_custom_call" | custom-call | tf_op jit(solution)/shard_map/attention_back/pallas_call | solution.py:434
  74.5 70.1 %reduce_terms.1 = (bf16[256,3584]{1,0:T(8,128)(2,1)}, bf16[256,7168]{1,0:T(8,128)(2,1)}, f32[2,224,512]{2,1,0:T(8,128)}) custom-call(bf16[7168,512]{1,0:T(8,128)(2,1)} %get-tuple-element.15.xt_in, bf16[32,224,512]{2,1,0:T(8,128)(2,1)} %get-tuple-element.16.w_in, bf16[1024,256]{1,0:T(8,128)(2,1)} %get-tuple-element.20.dkv_in, ...), custom_call_target="tpu_custom_call" | custom-call | tf_op jit(solution)/shard_map/reduce_terms/pallas_call | solution.py:738
  144.6 8.5 %update.1 = (bf16[256,3584]{1,0:T(8,128)(2,1)}, bf16[256,7168]{1,0:T(8,128)(2,1)}, f32[224,1024]{1,0:T(8,128)}, bf16[224,1024]{1,0:T(8,128)(2,1)}, bf16[224,1024]{1,0:T(8,128)(2,1)}) custom-call(bf16[256,3584]{1,0:T(8,128)(2,1)} %get-tuple-element.22.dq_in, bf16[256,7168]{1,0:T(8,128)(2,1)} %get-tuple-element.23.dn_in, ...), custom_call_target="tpu_custom_call" | custom-call | tf_op jit(solution)/shard_map/update/pallas_call | solution.py:802

commit v3 on v2

--- a/solution.py
+++ b/solution.py
@@ -17,10 +17,16 @@
 SHARDS = X * Y * ZH
 ROWS = D // SHARDS
 PARTS = (
-    (0, 80, ("x", "y"), True),
-    (80, 64, ("y", "x"), True),
-    (144, 32, ("x", "y"), False),
-    (176, 48, ("y", "x"), False),
+    (0, 96, ("x", "y"), True),
+    (96, 80, ("y", "x"), True),
+    (176, 16, ("x", "y"), False),
+    (192, 32, ("y", "x"), False),
+)
+SUM_PARTS = (
+    (0, 96, ("x", "y"), True),
+    (96, 80, ("y", "x"), True),
+    (176, 16, ("x", "y"), False),
+    (192, 32, ("y", "x"), False),
 )
 Z_FIRST = (0, 1)
 Z_LAST = (2, 3)
@@ -212,8 +218,8 @@
             second_from(p, 2, zr)
             over_z(p, 2, 0)
 
-    def forward_second(parts, zr):
-        for da in (0, -1, 1, 2):
+    def forward_second(parts, zr, after=None):
+        for k, da in enumerate((0, -1, 1, 2)):
             for p in parts:
                 b = PARTS[p][2][1]
                 for step in (1, -1):
@@ -225,6 +231,8 @@
                         here.along(b, step),
                     )
                     over_z(p, da, -step)
+            if after is not None:
+                after(k)
 
     def finish_second(parts, zr):
         for da in (0, -1, 1, 2):
@@ -276,8 +284,22 @@
     forward_second(Z_FIRST, 0)
     turn(42, 56)
     pending.append(local(xt, xt_out))
-    forward_second(Z_FIRST, 1)
     finish_second(Z_FIRST, 0)
+    acc[...] = jnp.zeros_like(acc)
+
+    def project(y, zh, cols, into):
+        at = pl.ds(pl.multiple_of((y * ZH + zh) * ROW_BLOCK, 128), ROW_BLOCK)
+        w_t = w[pl.ds((y * ZH + zh) * X, X), :, cols].reshape(ROW_BLOCK, HC)
+        acc[into] += dot(xs[:, at], w_t)
+
+    own_head = pl.ds(pl.multiple_of(zl * HC, HC), HC)
+    far_head = pl.ds(pl.multiple_of((1 - zl) * HC, HC), HC)
+
+    def own_half(k):
+        project(k, here.zh, far_head, 0)
+        project(k, here.zh, own_head, 1)
+
+    forward_second(Z_FIRST, 1, own_half)
     finish_second(Z_FIRST, 1)
     for p in Z_LAST:
         for da in (0, -1, 1, 2):
@@ -286,22 +308,16 @@
     pending.append(local(w, w_out))
 
     own_tokens = pl.ds(pl.multiple_of(zl * CT, CT), CT)
-    for far in (True, False):
-        head = 1 - zl if far else zl
-        cols = pl.ds(pl.multiple_of(head * HC, HC), HC)
-        acc[...] = jnp.zeros_like(acc)
-
-        @pl.loop(0, N_BLOCKS)
-        def _(t):
-            at = pl.ds(pl.multiple_of(t * ROW_BLOCK, 128), ROW_BLOCK)
-            w_t = w[pl.ds(t * X, X), :, cols].reshape(ROW_BLOCK, HC)
-            acc[...] += dot(xs[:, at], w_t)
-
-        if far:
-            kv[0] = acc[...].astype(BF16)
+    for into, cols in ((0, far_head), (1, own_head)):
+
+        @pl.loop(0, Y)
+        def _(y):
+            project(y, 1 - here.zh, cols, into)
+
+        kv[into] = acc[into].astype(BF16)
+        if into == 0:
             links.send("kv", kv.at[0], kv_out.at[own_tokens, :], here.partner())
         else:
-            kv[1] = acc[...].astype(BF16)
             pending.append(local(kv.at[1], kv_out.at[own_tokens, :]))
     own_q.wait()
     own_do.wait()
@@ -334,7 +350,7 @@
             pltpu.VMEM((D, CT), BF16),
             pltpu.VMEM((ROWS, COLS), F32),
             pltpu.VMEM((2, CT, HC), BF16),
-            pltpu.VMEM((CT, HC), F32),
+            pltpu.VMEM((2, CT, HC), F32),
             pltpu.VMEM(queries.shape, BF16),
             pltpu.VMEM(queries.shape, BF16),
             pltpu.VMEM((SEQ, QW), BF16),
@@ -352,7 +368,7 @@
 
 def attention_kernel(
     lengths, q_ref, do_ref, kv_ref, dq_ref, dkv_ref,
-    qs, dos, prob, dprob, dq_t, dk_acc, dv_acc,
+    qs, dos, prob, dprob, prob_half, d_scores, dk_acc, dv_acc,
 ):
     i = pl.program_id(0)
     scale = HEAD ** (-0.5)
@@ -369,9 +385,9 @@
         dk_acc[...] = jnp.zeros_like(dk_acc)
         dv_acc[...] = jnp.zeros_like(dv_acc)
 
-    lane = lax.broadcasted_iota(jnp.int32, (1, LANES), 1)
+    lane = lax.broadcasted_iota(jnp.int32, (1, CHUNK), 1)
     sub = lax.broadcasted_iota(jnp.int32, (CHUNK, 1), 0)
-    q_row = i * CHUNK + lax.rem(lane, CHUNK)
+    q_row = i * CHUNK + lane
     doc_start = jnp.zeros_like(q_row)
     first_start = jnp.int32(0)
     for e in ends:
@@ -382,47 +398,50 @@
     for a in range(GROUP):
         qs[a * CHUNK : (a + 1) * CHUNK, :] = q_ref[:, a * HEAD : (a + 1) * HEAD]
         dos[a * CHUNK : (a + 1) * CHUNK, :] = do_ref[:, a * HEAD : (a + 1) * HEAD]
-    dq_t[...] = jnp.zeros_like(dq_t)
-
-    def scores(j, top):
-        at = pl.ds(pl.multiple_of(j * CHUNK, CHUNK), CHUNK)
-        s = dot(kv_ref[at, 0:HEAD], qs[...], ((1,), (1,)))
-        k_row = j * CHUNK + sub
-        s = jnp.where((k_row >= doc_start) & (k_row <= q_row), s, -1e30)
-        prob[j - lowest] = s
-        return jnp.maximum(top, jnp.max(s, axis=0, keepdims=True))
-
-    top = lax.fori_loop(lowest, i + 1, scores, jnp.full((1, LANES), -3e38, F32))
-
-    def weigh(j, sums):
-        mass, delta = sums
-        at = pl.ds(pl.multiple_of(j * CHUNK, CHUNK), CHUNK)
-        p = jnp.exp2((prob[j - lowest] - top) * to_base2)
-        dp = dot(kv_ref[at, HEAD : 2 * HEAD], dos[...], ((1,), (1,)))
-        prob[j - lowest] = p
-        dprob[j - lowest] = dp
-        mass = mass + jnp.sum(p, axis=0, keepdims=True)
-        delta = delta + jnp.sum(p * dp, axis=0, keepdims=True)
-        return mass, delta
-
-    zero = jnp.zeros((1, LANES), F32)
-    mass, delta = lax.fori_loop(lowest, i + 1, weigh, (zero, zero))
-    inv = 1.0 / mass
-    delta = delta * inv
-
-    def back(j, carry):
-        at = pl.ds(pl.multiple_of(j * CHUNK, CHUNK), CHUNK)
-        p = prob[j - lowest] * inv
-        ds = (p * (dprob[j - lowest] - delta)).astype(BF16)
-        dv_acc[at, :] += dot(p.astype(BF16), dos[...])
-        dk_acc[at, :] += dot(ds, qs[...])
-        dq_t[...] += dot(kv_ref[at, 0:HEAD], ds, ((0,), (0,)))
-        return carry
-
-    lax.fori_loop(lowest, i + 1, back, 0)
-    for a in range(GROUP):
-        part = dq_t[:, a * CHUNK : (a + 1) * CHUNK].T * scale
-        dq_ref[:, a * HEAD : (a + 1) * HEAD] = part.astype(BF16)
+
+    def chunks(n):
+        low = i + 1 - n
+        keys = pl.ds(pl.multiple_of(low * CHUNK, CHUNK), n * CHUNK)
+        here = slice(0, n * CHUNK)
+        prob[here, :] = dot(kv_ref[keys, 0:HEAD], qs[...], ((1,), (1,)))
+        dprob[here, :] = dot(kv_ref[keys, HEAD : 2 * HEAD], dos[...], ((1,), (1,)))
+        for a in range(GROUP):
+            cols = slice(a * CHUNK, (a + 1) * CHUNK)
+            parts = []
+            top = None
+            for t in range(n):
+                k_row = (low + t) * CHUNK + sub
+                keep = k_row >= doc_start
+                if t == n - 1:
+                    keep = keep & (k_row <= q_row)
+                part = jnp.where(keep, prob[t * CHUNK : (t + 1) * CHUNK, cols], -1e30)
+                parts.append(part)
+                most = jnp.max(part, axis=0, keepdims=True)
+                top = most if top is None else jnp.maximum(top, most)
+            mass = jnp.zeros((1, CHUNK), F32)
+            delta = jnp.zeros((1, CHUNK), F32)
+            for t in range(n):
+                p = jnp.exp2((parts[t] - top) * to_base2)
+                parts[t] = p
+                mass = mass + jnp.sum(p, axis=0, keepdims=True)
+                dp = dprob[t * CHUNK : (t + 1) * CHUNK, cols]
+                delta = delta + jnp.sum(p * dp, axis=0, keepdims=True)
+            inv = 1.0 / mass
+            delta = delta * inv
+            for t in range(n):
+                rows = slice(t * CHUNK, (t + 1) * CHUNK)
+                p = parts[t] * inv
+                prob_half[rows, cols] = p.astype(BF16)
+                d_scores[rows, cols] = (p * (dprob[rows, cols] - delta)).astype(BF16)
+        dv_acc[keys, :] += dot(prob_half[here, :], dos[...])
+        dk_acc[keys, :] += dot(d_scores[here, :], qs[...])
+        dq_t = dot(kv_ref[keys, 0:HEAD], d_scores[here, :], ((0,), (0,)))
+        for a in range(GROUP):
+            part = dq_t[:, a * CHUNK : (a + 1) * CHUNK].T * scale
+            dq_ref[:, a * HEAD : (a + 1) * HEAD] = part.astype(BF16)
+
+    for n in range(1, N_CHUNKS + 1):
+        pl.when(i + 1 - lowest == n)(functools.partial(chunks, n))
 
     @pl.when(i == pl.num_programs(0) - 1)
     def _():
@@ -451,9 +470,10 @@
         scratch_shapes=[
             pltpu.VMEM((LANES, HEAD), BF16),
             pltpu.VMEM((LANES, HEAD), BF16),
-            pltpu.VMEM((N_CHUNKS, CHUNK, LANES), F32),
-            pltpu.VMEM((N_CHUNKS, CHUNK, LANES), F32),
-            pltpu.VMEM((HEAD, LANES), F32),
+            pltpu.VMEM((N_CHUNKS * CHUNK, LANES), F32),
+            pltpu.VMEM((N_CHUNKS * CHUNK, LANES), F32),
+            pltpu.VMEM((N_CHUNKS * CHUNK, LANES), BF16),
+            pltpu.VMEM((N_CHUNKS * CHUNK, LANES), BF16),
             pltpu.VMEM((SEQ, HEAD), F32),
             pltpu.VMEM((SEQ, HEAD), F32),
         ],
@@ -562,14 +582,14 @@
             ).astype(BF16)
 
     def rows_of(p):
-        return pl.ds(PARTS[p][0], PARTS[p][1])
+        return pl.ds(SUM_PARTS[p][0], SUM_PARTS[p][1])
 
     def term_at(at, p):
         zs = pl.ds(0, ZH) if p in Z_FIRST else pl.ds(own_z, 1)
         return term.at[at["y"], zs, at["x"], rows_of(p), :]
 
     def first_ring(p, k, off):
-        a, b = PARTS[p][2]
+        a, b = SUM_PARTS[p][2]
         opp, low, high = bufs[p][:3]
 
         def slot(da):
@@ -581,7 +601,7 @@
         )
 
     def second_ring(p):
-        a, b = PARTS[p][2]
+        a, b = SUM_PARTS[p][2]
         opp, low, high = bufs[p][3:]
 
         def slot(db):
@@ -592,7 +612,7 @@
     offs = (2, 1, -1, 0)
     rings = [[first_ring(p, k, off) for k, off in enumerate(offs)] for p in range(4)]
     finals = [second_ring(p) for p in range(4)]
-    late = pl.ds(PARTS[2][0], PARTS[2][1] + PARTS[3][1])
+    late = pl.ds(SUM_PARTS[2][0], SUM_PARTS[2][1] + SUM_PARTS[3][1])
 
     def make_terms(k):
         y = at_axis("y", offs[k])
@@ -724,7 +744,7 @@
 
 def reduce_terms(xt, w, dkv, dq):
     rings = []
-    for p, (_, rows, _, both) in enumerate(PARTS):
+    for p, (_, rows, _, both) in enumerate(SUM_PARTS):
         nz = ZH if both else 1
         rings += [
             pltpu.VMEM((4, 2, nz, rows, HC), BF16),
@@ -734,7 +754,7 @@
             pltpu.VMEM((nz, rows, COLS), BF16),
             pltpu.VMEM((nz, rows, COLS), BF16),
         ]
-    late = PARTS[2][1] + PARTS[3][1]
+    late = SUM_PARTS[2][1] + SUM_PARTS[3][1]
     return pl.pallas_call(
         reduce_kernel,
         out_shape=(
@@ -771,49 +791,67 @@
     )(xt, w, dkv, dq)
 
 
-STEPS = 7
-
-
 def update_kernel(
-    tokens, dq_in, dn_in, total, master, moment_one, moment_two,
+    tokens, dq_in, dn_in, total_in, master_in, one_in, two_in,
     dq_out, dn_out, master_out, one_out, two_out,
+    dq, dn, total, master, one, two, in_sem, out_sem,
 ):
-    dq_out[...] = dq_in[...]
-    dn_out[...] = dn_in[...]
-    for h in range(2):
-        cols = pl.ds(h * COLS, COLS)
-        grad = total[h] * float(tokens) ** (-0.5)
-        first = 0.9 * moment_one[:, cols].astype(F32) + 0.1 * grad
-        second = 0.999 * moment_two[:, cols].astype(F32) + 0.001 * grad * grad
-        master_out[:, cols] = master[:, cols] - 0.001 * (first / (1.0 - 0.9**3)) / (
-            jnp.sqrt(second / (1.0 - 0.999**3)) + 1e-08
-        )
-        one_out[:, cols] = first.astype(BF16)
-        two_out[:, cols] = second.astype(BF16)
+    gets, puts = [], []
+
+    def get(src, dst):
+        copy = pltpu.make_async_copy(src, dst, in_sem.at[len(gets)])
+        copy.start()
+        gets.append(copy)
+        return copy
+
+    def put(src, dst):
+        copy = pltpu.make_async_copy(src, dst, out_sem.at[len(puts)])
+        copy.start()
+        puts.append(copy)
+
+    first_gets = [get(total_in, total), get(master_in, master), get(one_in, one), get(two_in, two)]
+    blocks = []
+    for src, mid, dst, n in ((dn_in, dn, dn_out, 4), (dq_in, dq, dq_out, 2)):
+        rows = src.shape[0] // n
+        for b in range(n):
+            at = pl.ds(b * rows, rows)
+            blocks.append((get(src.at[at, :], mid.at[at, :]), mid.at[at, :], dst.at[at, :]))
+    for copy in first_gets:
+        copy.wait()
+    rows = ROWS // 2
+    for b in range(2):
+        at = pl.ds(b * rows, rows)
+        for h in range(2):
+            cols = pl.ds(h * COLS, COLS)
+            grad = total[h, at, :] * float(tokens) ** (-0.5)
+            first = 0.9 * one[at, cols].astype(F32) + 0.1 * grad
+            second = 0.999 * two[at, cols].astype(F32) + 0.001 * grad * grad
+            master[at, cols] = master[at, cols] - 0.001 * (first / (1.0 - 0.9**3)) / (
+                jnp.sqrt(second / (1.0 - 0.999**3)) + 1e-08
+            )
+            one[at, cols] = first.astype(BF16)
+            two[at, cols] = second.astype(BF16)
+        for mid, dst in ((master, master_out), (one, one_out), (two, two_out)):
+            put(mid.at[at, :], dst.at[at, :])
+        for copy, mid, dst in blocks[3 * b : 3 * b + 3]:
+            copy.wait()
+            put(mid, dst)
+    for copy in puts:
+        copy.wait()
 
 
 def update(tokens, dq, dn, total, master, moment_one, moment_two):
-    def across(a):
-        return pl.BlockSpec((a.shape[0], a.shape[1] // STEPS), lambda i: (0, i))
-
-    def down(a):
-        return pl.BlockSpec((a.shape[0] // STEPS, a.shape[1]), lambda i: (i, 0))
-
+    results = (dq, dn, master, moment_one, moment_two)
     return pl.pallas_call(
         functools.partial(update_kernel, tokens),
-        grid=(STEPS,),
-        out_shape=tuple(
-            jax.ShapeDtypeStruct(a.shape, a.dtype) for a in (dq, dn, master, moment_one, moment_two)
-        ),
-        in_specs=[
-            across(dq),
-            across(dn),
-            pl.BlockSpec((2, ROWS // STEPS, COLS), lambda i: (0, i, 0)),
-            down(master),
-            down(moment_one),
-            down(moment_two),
+        out_shape=tuple(jax.ShapeDtypeStruct(a.shape, a.dtype) for a in results),
+        in_specs=[ANY] * 6,
+        out_specs=(ANY,) * 5,
+        scratch_shapes=[
+            *[pltpu.VMEM(a.shape, a.dtype) for a in (dq, dn, total, master, moment_one, moment_two)],
+            pltpu.SemaphoreType.DMA((12,)),
+            pltpu.SemaphoreType.DMA((12,)),
         ],
-        out_specs=(across(dq), across(dn), down(master), down(moment_one), down(moment_two)),
         compiler_params=pltpu.CompilerParams(vmem_limit_bytes=VMEM_LIMIT),
         name="update",
     )(dq, dn, total, master, moment_one, moment_two)

time: 154 us -> 140 us (0.909)
  Pallas kernels: 152 us -> 139 us
    pallas_call x1, Pallas kernels: 70.1 us -> 66 us  [reduce_terms(): pl.pallas_call(reduce_kernel, out_shape=(jax.ShapeDtypeStruct((TOK, 4 * Q...]
    pallas_call x1, Pallas kernels: 19.3 us -> 15.3 us  [attention(): pl.pallas_call(attention_kernel, grid=(SEQ // CHUNK,), out_shape=(jax.Sha...]
    pallas_call x1, Pallas kernels: 8.53 us -> 5.33 us  [update(): pl.pallas_call(functools.partial(update_kernel, tokens), out_shape=tuple(...]
    pallas_call x1, Pallas kernels: 54.5 us -> 52.5 us  [gather(): pl.pallas_call(gather_kernel, out_shape=(jax.ShapeDtypeStruct((SHARDS, RO...]
where the time goes in v3:
time: 140 us
  Pallas kernels  139 us (99%)
    pallas_call x1, Pallas kernels, reduce_terms(): pl.pallas_call(reduce_kernel, out_shape=(jax.ShapeDtypeStruct((TOK, 4 * Q...  66 us
    pallas_call x1, Pallas kernels, gather(): pl.pallas_call(gather_kernel, out_shape=(jax.ShapeDtypeStruct((SHARDS, RO...  52.5 us
    pallas_call x1, Pallas kernels, attention(): pl.pallas_call(attention_kernel, grid=(SEQ // CHUNK,), out_shape=(jax.Sha...  15.3 us
    pallas_call x1, Pallas kernels, update(): pl.pallas_call(functools.partial(update_kernel, tokens), out_shape=tuple(...  5.33 us

profile of v3, /device:TPU:1, one launch (start us, length us, event | category | flops | bytes accessed | tf_op | source)
XLA Modules:
  0.0 139.9 jit_solution(9736095748531316446)
XLA Ops:
  0.6 52.5 %gather_project.1 = (bf16[32,224,512]{2,1,0:T(8,128)(2,1)}, bf16[7168,512]{1,0:T(8,128)(2,1)}, bf16[1024,896]{1,0:T(8,128)(2,1)}, bf16[1024,896]{1,0:T(8,128)(2,1)}, bf16[1024,256]{1,0:T(8,128)(2,1)}) custom-call(bf16[256,7168]{1,0:T(8,128)(2,1)} %normed.1, bf16[256,3584]{1,0:T(8,128)(2,1)} %queries.1, bf16[256,3584]{1,0:T(8,128)(2,1)} %out_grad.1, ...), custom_call_target="tpu_custom_call" | custom-call | tf_op jit(solution)/shard_map/gather_project/pallas_call | solution.py:336
  53.1 15.3 %attention_back.1 = (bf16[1024,896]{1,0:T(8,128)(2,1)}, bf16[1024,256]{1,0:T(8,128)(2,1)}) custom-call(s32[1,8]{1,0:T(1,128)} %lengths.1, bf16[1024,896]{1,0:T(8,128)(2,1)} %get-tuple-element.17.q_ref, bf16[1024,896]{1,0:T(8,128)(2,1)} %get-tuple-element.18.do_ref, bf16[1024,256]{1,0:T(8,128)(2,1)} %get-tuple-element.19.kv_ref), custom_call_target="tpu_custom_call" | custom-call | tf_op jit(solution)/shard_map/attention_back/pallas_call | solution.py:453
  68.4 66.0 %reduce_terms.1 = (bf16[256,3584]{1,0:T(8,128)(2,1)}, bf16[256,7168]{1,0:T(8,128)(2,1)}, f32[2,224,512]{2,1,0:T(8,128)}) custom-call(bf16[7168,512]{1,0:T(8,128)(2,1)} %get-tuple-element.15.xt_in, bf16[32,224,512]{2,1,0:T(8,128)(2,1)} %get-tuple-element.16.w_in, bf16[1024,256]{1,0:T(8,128)(2,1)} %get-tuple-element.20.dkv_in, ...), custom_call_target="tpu_custom_call" | custom-call | tf_op jit(solution)/shard_map/reduce_terms/pallas_call | solution.py:758
  134.4 5.3 %update.1 = (bf16[256,3584]{1,0:T(8,128)(2,1)}, bf16[256,7168]{1,0:T(8,128)(2,1)}, f32[224,1024]{1,0:T(8,128)}, bf16[224,1024]{1,0:T(8,128)(2,1)}, bf16[224,1024]{1,0:T(8,128)(2,1)}) custom-call(bf16[256,3584]{1,0:T(8,128)(2,1)} %get-tuple-element.22.dq_in, bf16[256,7168]{1,0:T(8,128)(2,1)} %get-tuple-element.23.dn_in, ...), custom_call_target="tpu_custom_call" | custom-call | tf_op jit(solution)/shard_map/update/pallas_call | solution.py:845

commit v4 on v3

--- a/solution.py
+++ b/solution.py
@@ -23,9 +23,9 @@
     (192, 32, ("y", "x"), False),
 )
 SUM_PARTS = (
-    (0, 96, ("x", "y"), True),
-    (96, 80, ("y", "x"), True),
-    (176, 16, ("x", "y"), False),
+    (0, 80, ("x", "y"), True),
+    (80, 80, ("y", "x"), True),
+    (160, 32, ("x", "y"), False),
     (192, 32, ("y", "x"), False),
 )
 Z_FIRST = (0, 1)
@@ -97,10 +97,14 @@
     def __init__(self, send_sem, recv_sem, place):
         self.send_sem, self.recv_sem, self.place = send_sem, recv_sem, place
         self.index = {}
+        self.used = 0
         self.sent = []
 
-    def _copy(self, key, src, dst, dev):
-        k = self.index.setdefault(key, len(self.index))
+    def _copy(self, key, src, dst, dev, half=None):
+        if key not in self.index:
+            self.index[key] = self.used
+            self.used += 1 if half is None else 2
+        k = self.index[key] + (0 if half is None else half)
         return pltpu.make_async_remote_copy(
             src_ref=src,
             dst_ref=dst,
@@ -110,13 +114,13 @@
             device_id_type=MESH,
         )
 
-    def send(self, key, src, dst, dev):
-        copy = self._copy(key, src, dst, dev)
+    def send(self, key, src, dst, dev, half=None):
+        copy = self._copy(key, src, dst, dev, half)
         copy.start()
         self.sent.append(copy)
 
-    def recv(self, key, dst):
-        self._copy(key, dst, dst, self.place.other_core()).wait_recv()
+    def recv(self, key, dst, half=None):
+        self._copy(key, dst, dst, self.place.other_core(), half).wait_recv()
 
     def drain(self):
         for copy in self.sent:
@@ -491,8 +495,8 @@
     xt, w, term, dkv, dq_src, dq_all, z_early, z_in, l_in, mine, total, dn_send, dn_recv, dn_own,
     *rest,
 ):
-    bufs = [rest[6 * p : 6 * p + 6] for p in range(4)]
-    send_sem, recv_sem, loc_sem = rest[24:]
+    bufs = [rest[4 * p : 4 * p + 4] for p in range(4)]
+    send_sem, recv_sem, loc_sem = rest[16:]
     here = Place()
     links = Links(send_sem, recv_sem, here)
     n_local = [0]
@@ -517,7 +521,12 @@
         return pl.ds(pl.multiple_of((core_of * 2 + zl_of) * QW, 128), QW)
 
     get_dkv = local(dkv_in.at[own_tokens, :], dkv.at[zl])
-    get_xt = local(xt_in, xt)
+    offs = (2, 1, -1, 0)
+    get_xt = []
+    for off in offs:
+        y = lax.rem(here.y + off + Y, Y)
+        at = pl.ds(pl.multiple_of(y * ZH * ROW_BLOCK, 128), ZH * ROW_BLOCK)
+        get_xt.append(local(xt_in.at[at, :], xt.at[at, :]))
     get_dq = local(dq_in, dq_src)
     own_dq = local(dq_in.at[seq_rows(here.sq), :], dq_all.at[:, head_cols(zl, core)])
     here.greet()
@@ -525,8 +534,6 @@
     get_w = local(w_in, w)
     pending = []
     get_dkv.wait()
-    get_xt.wait()
-    links.recv("dkv", dkv.at[1 - zl])
 
     pos = {"x": here.x, "y": here.y}
     size = {"x": X, "y": Y}
@@ -535,50 +542,49 @@
         return lax.rem(pos[axis] + off + size[axis], size[axis])
 
     class Ring:
-        def __init__(self, name, axis, slot, opp, low, high):
+        def __init__(self, name, axis, slot, opp, land):
             self.name, self.axis, self.slot = name, axis, slot
-            self.opp, self.low, self.high = opp, low, high
+            self.opp, self.land = opp, land
 
         def half(self, ref, h):
-            return ref.at[:, :, pl.ds(h * HC, HC)]
-
-        def send_far(self):
-            for h, step in ((0, 1), (1, -1)):
-                links.send(
-                    (self.name, "far", step),
-                    self.half(self.slot(2), h), self.opp(h), here.along(self.axis, step),
-                )
-
-        def send_near(self, step):
-            h, land = (1, self.low) if step == 1 else (0, self.high)
+            start = h * HC if isinstance(h, int) else pl.multiple_of(h * HC, HC)
+            return ref.at[:, :, pl.ds(start, HC)]
+
+        def send_far(self, h):
             links.send(
-                (self.name, "near", step),
-                self.half(self.slot(step), h), self.half(land(), h), here.along(self.axis, step),
+                (self.name, "far"),
+                self.half(self.slot(2), h), self.opp(h), here.along(self.axis, 1 - 2 * h), h,
+            )
+
+        def send_near(self, h):
+            step = 2 * h - 1
+            links.send(
+                (self.name, "near"),
+                self.half(self.slot(step), h), self.half(self.land(1 - h), h),
+                here.along(self.axis, step), h,
             )
 
         def forward(self):
             for h, step in ((0, 1), (1, -1)):
-                links.recv((self.name, "far", step), self.opp(h))
+                links.recv((self.name, "far"), self.opp(h), h)
                 here_sum = self.half(self.slot(step), h)
                 here_sum[...] = (
                     here_sum[...].astype(F32) + self.opp(h)[...].astype(F32)
                 ).astype(BF16)
-                land = self.low if step == 1 else self.high
                 links.send(
-                    (self.name, "sum", step),
-                    here_sum, self.half(land(), h), here.along(self.axis, step),
+                    (self.name, "sum"),
+                    here_sum, self.half(self.land(h), h), here.along(self.axis, step), h,
                 )
 
         def finish(self):
-            for h, step in ((1, 1), (0, -1)):
-                land = self.low if step == 1 else self.high
-                links.recv((self.name, "near", step), self.half(land(), h))
-                links.recv((self.name, "sum", step), self.half(land(), 1 - h))
+            for h in range(2):
+                links.recv((self.name, "near"), self.half(self.land(1 - h), h), h)
+                links.recv((self.name, "sum"), self.half(self.land(h), h), h)
             mine_ref = self.slot(0)
             mine_ref[...] = (
                 mine_ref[...].astype(F32)
-                + self.low()[...].astype(F32)
-                + self.high()[...].astype(F32)
+                + self.land(0)[...].astype(F32)
+                + self.land(1)[...].astype(F32)
             ).astype(BF16)
 
     def rows_of(p):
@@ -590,56 +596,56 @@
 
     def first_ring(p, k, off):
         a, b = SUM_PARTS[p][2]
-        opp, low, high = bufs[p][:3]
+        opp, land = bufs[p][:2]
 
         def slot(da):
             return term_at({a: at_axis(a, da), b: at_axis(b, off)}, p)
 
         return Ring(
             ("first", p, k), a, slot,
-            lambda h: opp.at[k, h], lambda: low.at[k], lambda: high.at[k],
+            lambda h: opp.at[k, h], lambda side: land.at[k, side],
         )
 
     def second_ring(p):
         a, b = SUM_PARTS[p][2]
-        opp, low, high = bufs[p][3:]
+        opp, land = bufs[p][2:]
 
         def slot(db):
             return term_at({a: pos[a], b: at_axis(b, db)}, p)
 
-        return Ring(("second", p), b, slot, lambda h: opp.at[h], lambda: low, lambda: high)
-
-    offs = (2, 1, -1, 0)
+        return Ring(("second", p), b, slot, lambda h: opp.at[h], lambda side: land.at[side])
+
     rings = [[first_ring(p, k, off) for k, off in enumerate(offs)] for p in range(4)]
     finals = [second_ring(p) for p in range(4)]
     late = pl.ds(SUM_PARTS[2][0], SUM_PARTS[2][1] + SUM_PARTS[3][1])
 
-    def make_terms(k):
+    def make_terms(k, h):
         y = at_axis("y", offs[k])
+        cols = pl.ds(pl.multiple_of(h * HC, HC), HC)
         for z in (far_z, own_z):
             at = pl.ds(pl.multiple_of((y * ZH + z) * ROW_BLOCK, 128), ROW_BLOCK)
-            for h in range(2):
-                t = dot(xt[at, :], dkv[h]).astype(BF16)
-                term[y, z, :, :, h * HC : (h + 1) * HC] = t.reshape(X, ROWS, HC)
+            t = dot(xt[at, :], dkv[h]).astype(BF16)
+            term[y, z, :, :, cols] = t.reshape(X, ROWS, HC)
         links.send(
-            ("early", k), term.at[y, far_z, :, late, :], z_early.at[k], here.cross()
+            ("early", k),
+            term.at[y, far_z, :, late, cols], z_early.at[k, :, :, cols], here.cross(), h,
         )
 
     def add_early(k):
         y = at_axis("y", offs[k])
-        links.recv(("early", k), z_early.at[k])
+        for h in range(2):
+            links.recv(("early", k), z_early.at[k, :, :, pl.ds(h * HC, HC)], h)
         into = term.at[y, own_z, :, late, :]
         into[...] = (into[...].astype(F32) + z_early[k].astype(F32)).astype(BF16)
 
-    def launch(k, p_x, p_y):
-        rings[p_x][k].send_far()
-        for step in (1, -1):
-            rings[p_x][k].send_near(step)
+    def launch(k, p_x, p_y, h):
+        rings[p_x][k].send_far(h)
+        rings[p_x][k].send_near(h)
         for piece in rings[p_y]:
             if k == 0:
-                piece.send_far()
-            elif k < 3:
-                piece.send_near(offs[k])
+                piece.send_far(h)
+            elif k == 2:
+                piece.send_near(h)
 
     def dn_far(t):
         at = pl.ds(t * ROW_BLOCK, ROW_BLOCK)
@@ -661,8 +667,13 @@
         pending.append(local(dn_own.at[:, at], dn_out.at[:, at]))
 
     for k in range(4):
-        make_terms(k)
-        launch(k, 0, 1)
+        get_xt[k].wait()
+        make_terms(k, zl)
+        launch(k, 0, 1, zl)
+    links.recv("dkv", dkv.at[1 - zl])
+    for k in range(4):
+        make_terms(k, 1 - zl)
+        launch(k, 0, 1, 1 - zl)
     get_dq.wait()
     others = (("p", 1 - zl, core), ("c", zl, 1 - core), ("d", 1 - zl, 1 - core))
     for way, zl_to, core_to in others:
@@ -676,17 +687,19 @@
         for p in Z_FIRST:
             rings[p][k].forward()
         add_early(k)
-        launch(k, 2, 3)
+        for h in range(2):
+            launch(k, 2, 3, h)
         dn_far(2 * k)
         dn_far(2 * k + 1)
 
     def end_first(k, parts):
         for p in parts:
             rings[p][k].finish()
-            if k == 0:
-                finals[p].send_far()
-            elif k < 3:
-                finals[p].send_near(offs[k])
+            for h in range(2):
+                if k == 0:
+                    finals[p].send_far(h)
+                elif k < 3 and offs[k] == 2 * h - 1:
+                    finals[p].send_near(h)
 
     for k in range(4):
         for p in Z_LAST:
@@ -748,11 +761,9 @@
         nz = ZH if both else 1
         rings += [
             pltpu.VMEM((4, 2, nz, rows, HC), BF16),
-            pltpu.VMEM((4, nz, rows, COLS), BF16),
-            pltpu.VMEM((4, nz, rows, COLS), BF16),
+            pltpu.VMEM((4, 2, nz, rows, COLS), BF16),
             pltpu.VMEM((2, nz, rows, HC), BF16),
-            pltpu.VMEM((nz, rows, COLS), BF16),
-            pltpu.VMEM((nz, rows, COLS), BF16),
+            pltpu.VMEM((2, nz, rows, COLS), BF16),
         ]
     late = SUM_PARTS[2][1] + SUM_PARTS[3][1]
     return pl.pallas_call(

time: 140 us -> 131 us (0.936)
  Pallas kernels: 139 us -> 130 us
    pallas_call x1, Pallas kernels: 66 us -> 57.1 us  [reduce_terms(): pl.pallas_call(reduce_kernel, out_shape=(jax.ShapeDtypeStruct((TOK, 4 * Q...]
where the time goes in v4:
time: 131 us
  Pallas kernels  130 us (99%)
    pallas_call x1, Pallas kernels, reduce_terms(): pl.pallas_call(reduce_kernel, out_shape=(jax.ShapeDtypeStruct((TOK, 4 * Q...  57.1 us
    pallas_call x1, Pallas kernels, gather(): pl.pallas_call(gather_kernel, out_shape=(jax.ShapeDtypeStruct((SHARDS, RO...  52.5 us
    pallas_call x1, Pallas kernels, attention(): pl.pallas_call(attention_kernel, grid=(SEQ // CHUNK,), out_shape=(jax.Sha...  15 us
    pallas_call x1, Pallas kernels, update(): pl.pallas_call(functools.partial(update_kernel, tokens), out_shape=tuple(...  5.33 us

profile of v4, /device:TPU:1, one launch (start us, length us, event | category | flops | bytes accessed | tf_op | source)
XLA Modules:
  0.0 130.7 jit_solution(16150623692986448515)
XLA Ops:
  0.6 52.5 %gather_project.1 = (bf16[32,224,512]{2,1,0:T(8,128)(2,1)}, bf16[7168,512]{1,0:T(8,128)(2,1)}, bf16[1024,896]{1,0:T(8,128)(2,1)}, bf16[1024,896]{1,0:T(8,128)(2,1)}, bf16[1024,256]{1,0:T(8,128)(2,1)}) custom-call(bf16[256,7168]{1,0:T(8,128)(2,1)} %normed.1, bf16[256,3584]{1,0:T(8,128)(2,1)} %queries.1, bf16[256,3584]{1,0:T(8,128)(2,1)} %out_grad.1, ...), custom_call_target="tpu_custom_call" | custom-call | tf_op jit(solution)/shard_map/gather_project/pallas_call | solution.py:340
  53.1 15.0 %attention_back.1 = (bf16[1024,896]{1,0:T(8,128)(2,1)}, bf16[1024,256]{1,0:T(8,128)(2,1)}) custom-call(s32[1,8]{1,0:T(1,128)} %lengths.1, bf16[1024,896]{1,0:T(8,128)(2,1)} %get-tuple-element.17.q_ref, bf16[1024,896]{1,0:T(8,128)(2,1)} %get-tuple-element.18.do_ref, bf16[1024,256]{1,0:T(8,128)(2,1)} %get-tuple-element.19.kv_ref), custom_call_target="tpu_custom_call" | custom-call | tf_op jit(solution)/shard_map/attention_back/pallas_call | solution.py:457
  68.1 57.1 %reduce_terms.1 = (bf16[256,3584]{1,0:T(8,128)(2,1)}, bf16[256,7168]{1,0:T(8,128)(2,1)}, f32[2,224,512]{2,1,0:T(8,128)}) custom-call(bf16[7168,512]{1,0:T(8,128)(2,1)} %get-tuple-element.15.xt_in, bf16[32,224,512]{2,1,0:T(8,128)(2,1)} %get-tuple-element.16.w_in, bf16[1024,256]{1,0:T(8,128)(2,1)} %get-tuple-element.20.dkv_in, ...), custom_call_target="tpu_custom_call" | custom-call | tf_op jit(solution)/shard_map/reduce_terms/pallas_call | solution.py:769
  125.2 5.3 %update.1 = (bf16[256,3584]{1,0:T(8,128)(2,1)}, bf16[256,7168]{1,0:T(8,128)(2,1)}, f32[224,1024]{1,0:T(8,128)}, bf16[224,1024]{1,0:T(8,128)(2,1)}, bf16[224,1024]{1,0:T(8,128)(2,1)}) custom-call(bf16[256,3584]{1,0:T(8,128)(2,1)} %get-tuple-element.22.dq_in, bf16[256,7168]{1,0:T(8,128)(2,1)} %get-tuple-element.23.dn_in, ...), custom_call_target="tpu_custom_call" | custom-call | tf_op jit(solution)/shard_map/update/pallas_call | solution.py:856

commit v5 on v4

--- a/solution.py
+++ b/solution.py
@@ -90,7 +90,10 @@
         near.append(self.dev(zl=1 - self.zl, core=1 - self.core))
         for d in near:
             pl.semaphore_signal(barrier, inc=1, device_id=d, device_id_type=MESH)
-        pl.semaphore_wait(barrier, len(near))
+        return len(near)
+
+    def all_in(self, count):
+        pl.semaphore_wait(pltpu.get_barrier_semaphore(), count)
 
 
 class Links:
@@ -163,9 +166,25 @@
     own_q = local(queries.at[:, head_cols(zl, core)], q_all.at[seq_rows(here.sq), :])
     own_do = local(out_grad.at[:, head_cols(zl, core)], do_all.at[seq_rows(here.sq), :])
     pending = []
-    here.greet()
+    count = here.greet()
+    own = (here.y * ZH + here.zh) * X + here.x
     get_master.wait()
-
+    w[own] = mas[...].astype(BF16)
+    get_q.wait()
+    get_do.wait()
+    here.all_in(count)
+    others = (("p", 1 - zl, core), ("d", 1 - zl, 1 - core), ("c", zl, 1 - core))
+
+    def send_heads(ways):
+        for name, src, dst in (("q", q_src, q_all), ("do", do_src, do_all)):
+            for way, zl_to, core_to in ways:
+                links.send(
+                    (name, way),
+                    src.at[:, head_cols(zl_to, core_to)], dst.at[seq_rows(here.sq), :],
+                    here.dev(zl=zl_to, core=core_to),
+                )
+
+    send_heads(others[:2])
     pos = {"x": here.x, "y": here.y}
     size = {"x": X, "y": Y}
 
@@ -179,9 +198,6 @@
         s = (at["y"] * ZH + zh) * X + at["x"]
         cols = pl.ds(0, COLS) if half is None else pl.ds(half * HC, HC)
         return w.at[s, pl.ds(row, rows), cols]
-
-    own = (here.y * ZH + here.zh) * X + here.x
-    w[own] = mas[...].astype(BF16)
 
     def send(key, ref, dev):
         links.send(key, ref, ref, dev)
@@ -259,16 +275,7 @@
     for p in Z_LAST:
         over_z(p, 0, 0)
     links.send("normed", normed, xs.at[own_rows, :], here.other_core())
-    get_q.wait()
-    get_do.wait()
-    others = (("p", 1 - zl, core), ("c", zl, 1 - core), ("d", 1 - zl, 1 - core))
-    for name, src, dst in (("q", q_src, q_all), ("do", do_src, do_all)):
-        for way, zl_to, core_to in others:
-            links.send(
-                (name, way),
-                src.at[:, head_cols(zl_to, core_to)], dst.at[seq_rows(here.sq), :],
-                here.dev(zl=zl_to, core=core_to),
-            )
+    send_heads(others[2:])
     forward_first(Z_LAST, 0)
     forward_first(Z_FIRST, 0)
     finish_first(Z_LAST, 0)
@@ -441,8 +448,8 @@
         dk_acc[keys, :] += dot(d_scores[here, :], qs[...])
         dq_t = dot(kv_ref[keys, 0:HEAD], d_scores[here, :], ((0,), (0,)))
         for a in range(GROUP):
-            part = dq_t[:, a * CHUNK : (a + 1) * CHUNK].T * scale
-            dq_ref[:, a * HEAD : (a + 1) * HEAD] = part.astype(BF16)
+            part = (dq_t[:, a * CHUNK : (a + 1) * CHUNK] * scale).astype(BF16)
+            dq_ref[:, a * HEAD : (a + 1) * HEAD] = part.T
 
     for n in range(1, N_CHUNKS + 1):
         pl.when(i + 1 - lowest == n)(functools.partial(chunks, n))
@@ -529,8 +536,7 @@
         get_xt.append(local(xt_in.at[at, :], xt.at[at, :]))
     get_dq = local(dq_in, dq_src)
     own_dq = local(dq_in.at[seq_rows(here.sq), :], dq_all.at[:, head_cols(zl, core)])
-    here.greet()
-    links.send("dkv", dkv_in.at[far_tokens, :], dkv.at[zl], here.partner())
+    count = here.greet()
     get_w = local(w_in, w)
     pending = []
     get_dkv.wait()
@@ -626,6 +632,10 @@
             at = pl.ds(pl.multiple_of((y * ZH + z) * ROW_BLOCK, 128), ROW_BLOCK)
             t = dot(xt[at, :], dkv[h]).astype(BF16)
             term[y, z, :, :, cols] = t.reshape(X, ROWS, HC)
+
+    def send_early(k, h):
+        y = at_axis("y", offs[k])
+        cols = pl.ds(pl.multiple_of(h * HC, HC), HC)
         links.send(
             ("early", k),
             term.at[y, far_z, :, late, cols], z_early.at[k, :, :, cols], here.cross(), h,
@@ -669,10 +679,15 @@
     for k in range(4):
         get_xt[k].wait()
         make_terms(k, zl)
+        if k == 0:
+            here.all_in(count)
+            links.send("dkv", dkv_in.at[far_tokens, :], dkv.at[zl], here.partner())
+        send_early(k, zl)
         launch(k, 0, 1, zl)
     links.recv("dkv", dkv.at[1 - zl])
     for k in range(4):
         make_terms(k, 1 - zl)
+        send_early(k, 1 - zl)
         launch(k, 0, 1, 1 - zl)
     get_dq.wait()
     others = (("p", 1 - zl, core), ("c", zl, 1 - core), ("d", 1 - zl, 1 - core))

time: 131 us -> 131 us (level)
  no operation moved by 1% of the time
where the time goes in v5:
time: 131 us
  Pallas kernels  130 us (99%)
    pallas_call x1, Pallas kernels, reduce_terms(): pl.pallas_call(reduce_kernel, out_shape=(jax.ShapeDtypeStruct((TOK, 4 * Q...  57.6 us
    pallas_call x1, Pallas kernels, gather(): pl.pallas_call(gather_kernel, out_shape=(jax.ShapeDtypeStruct((SHARDS, RO...  52.3 us
    pallas_call x1, Pallas kernels, attention(): pl.pallas_call(attention_kernel, grid=(SEQ // CHUNK,), out_shape=(jax.Sha...  14.5 us
    pallas_call x1, Pallas kernels, update(): pl.pallas_call(functools.partial(update_kernel, tokens), out_shape=tuple(...  5.33 us

profile of v5, /device:TPU:1, one launch (start us, length us, event | category | flops | bytes accessed | tf_op | source)
XLA Modules:
  0.0 130.5 jit_solution(17578449484678218394)
XLA Ops:
  0.6 52.3 %gather_project.1 = (bf16[32,224,512]{2,1,0:T(8,128)(2,1)}, bf16[7168,512]{1,0:T(8,128)(2,1)}, bf16[1024,896]{1,0:T(8,128)(2,1)}, bf16[1024,896]{1,0:T(8,128)(2,1)}, bf16[1024,256]{1,0:T(8,128)(2,1)}) custom-call(bf16[256,7168]{1,0:T(8,128)(2,1)} %normed.1, bf16[256,3584]{1,0:T(8,128)(2,1)} %queries.1, bf16[256,3584]{1,0:T(8,128)(2,1)} %out_grad.1, ...), custom_call_target="tpu_custom_call" | custom-call | tf_op jit(solution)/shard_map/gather_project/pallas_call | solution.py:347
  52.9 14.5 %attention_back.1 = (bf16[1024,896]{1,0:T(8,128)(2,1)}, bf16[1024,256]{1,0:T(8,128)(2,1)}) custom-call(s32[1,8]{1,0:T(1,128)} %lengths.1, bf16[1024,896]{1,0:T(8,128)(2,1)} %get-tuple-element.17.q_ref, bf16[1024,896]{1,0:T(8,128)(2,1)} %get-tuple-element.18.do_ref, bf16[1024,256]{1,0:T(8,128)(2,1)} %get-tuple-element.19.kv_ref), custom_call_target="tpu_custom_call" | custom-call | tf_op jit(solution)/shard_map/attention_back/pallas_call | solution.py:464
  67.5 57.6 %reduce_terms.1 = (bf16[256,3584]{1,0:T(8,128)(2,1)}, bf16[256,7168]{1,0:T(8,128)(2,1)}, f32[2,224,512]{2,1,0:T(8,128)}) custom-call(bf16[7168,512]{1,0:T(8,128)(2,1)} %get-tuple-element.15.xt_in, bf16[32,224,512]{2,1,0:T(8,128)(2,1)} %get-tuple-element.16.w_in, bf16[1024,256]{1,0:T(8,128)(2,1)} %get-tuple-element.20.dkv_in, ...), custom_call_target="tpu_custom_call" | custom-call | tf_op jit(solution)/shard_map/reduce_terms/pallas_call | solution.py:784
  125.0 5.3 %update.1 = (bf16[256,3584]{1,0:T(8,128)(2,1)}, bf16[256,7168]{1,0:T(8,128)(2,1)}, f32[224,1024]{1,0:T(8,128)}, bf16[224,1024]{1,0:T(8,128)(2,1)}, bf16[224,1024]{1,0:T(8,128)(2,1)}) custom-call(bf16[256,3584]{1,0:T(8,128)(2,1)} %get-tuple-element.22.dq_in, bf16[256,7168]{1,0:T(8,128)(2,1)} %get-tuple-element.23.dn_in, ...), custom_call_target="tpu_custom_call" | custom-call | tf_op jit(solution)/shard_map/update/pallas_call | solution.py:871

commit v6 on v5

--- a/solution.py
+++ b/solution.py
@@ -835,13 +835,18 @@
         copy.start()
         puts.append(copy)
 
-    first_gets = [get(total_in, total), get(master_in, master), get(one_in, one), get(two_in, two)]
+    adam = ((total_in, total), (master_in, master), (one_in, one), (two_in, two))
     blocks = []
     for src, mid, dst, n in ((dn_in, dn, dn_out, 4), (dq_in, dq, dq_out, 2)):
         rows = src.shape[0] // n
         for b in range(n):
             at = pl.ds(b * rows, rows)
             blocks.append((get(src.at[at, :], mid.at[at, :]), mid.at[at, :], dst.at[at, :]))
+            if len(blocks) == 2:
+                first_gets = [get(near, far) for near, far in adam]
+    for copy, mid, dst in blocks[:2]:
+        copy.wait()
+        put(mid, dst)
     for copy in first_gets:
         copy.wait()
     rows = ROWS // 2
@@ -859,7 +864,7 @@
             two[at, cols] = second.astype(BF16)
         for mid, dst in ((master, master_out), (one, one_out), (two, two_out)):
             put(mid.at[at, :], dst.at[at, :])
-        for copy, mid, dst in blocks[3 * b : 3 * b + 3]:
+        for copy, mid, dst in blocks[2 * b + 2 : 2 * b + 4]:
             copy.wait()
             put(mid, dst)
     for copy in puts:

time: 131 us -> 131 us (level)
  no operation moved by 1% of the time
where the time goes in v6:
time: 131 us; the launch traced here: 130 us
  Pallas kernels  130 us (99%)
    pallas_call x1, Pallas kernels, reduce_terms(): pl.pallas_call(reduce_kernel, out_shape=(jax.ShapeDtypeStruct((TOK, 4 * Q...  58.3 us
    pallas_call x1, Pallas kernels, gather(): pl.pallas_call(gather_kernel, out_shape=(jax.ShapeDtypeStruct((SHARDS, RO...  52.3 us
    pallas_call x1, Pallas kernels, attention(): pl.pallas_call(attention_kernel, grid=(SEQ // CHUNK,), out_shape=(jax.Sha...  13.3 us
    pallas_call x1, Pallas kernels, update(): pl.pallas_call(functools.partial(update_kernel, tokens), out_shape=tuple(...  5.81 us

profile of v6, /device:TPU:1, one launch (start us, length us, event | category | flops | bytes accessed | tf_op | source)
XLA Modules:
  0.0 130.5 jit_solution(7585780122738530725)
XLA Ops:
  0.6 52.3 %gather_project.1 = (bf16[32,224,512]{2,1,0:T(8,128)(2,1)}, bf16[7168,512]{1,0:T(8,128)(2,1)}, bf16[1024,896]{1,0:T(8,128)(2,1)}, bf16[1024,896]{1,0:T(8,128)(2,1)}, bf16[1024,256]{1,0:T(8,128)(2,1)}) custom-call(bf16[256,7168]{1,0:T(8,128)(2,1)} %normed.1, bf16[256,3584]{1,0:T(8,128)(2,1)} %queries.1, bf16[256,3584]{1,0:T(8,128)(2,1)} %out_grad.1, ...), custom_call_target="tpu_custom_call" | custom-call | tf_op jit(solution)/shard_map/gather_project/pallas_call | solution.py:347
  52.9 13.3 %attention_back.1 = (bf16[1024,896]{1,0:T(8,128)(2,1)}, bf16[1024,256]{1,0:T(8,128)(2,1)}) custom-call(s32[1,8]{1,0:T(1,128)} %lengths.1, bf16[1024,896]{1,0:T(8,128)(2,1)} %get-tuple-element.17.q_ref, bf16[1024,896]{1,0:T(8,128)(2,1)} %get-tuple-element.18.do_ref, bf16[1024,256]{1,0:T(8,128)(2,1)} %get-tuple-element.19.kv_ref), custom_call_target="tpu_custom_call" | custom-call | tf_op jit(solution)/shard_map/attention_back/pallas_call | solution.py:464
  66.2 58.3 %reduce_terms.1 = (bf16[256,3584]{1,0:T(8,128)(2,1)}, bf16[256,7168]{1,0:T(8,128)(2,1)}, f32[2,224,512]{2,1,0:T(8,128)}) custom-call(bf16[7168,512]{1,0:T(8,128)(2,1)} %get-tuple-element.15.xt_in, bf16[32,224,512]{2,1,0:T(8,128)(2,1)} %get-tuple-element.16.w_in, bf16[1024,256]{1,0:T(8,128)(2,1)} %get-tuple-element.20.dkv_in, ...), custom_call_target="tpu_custom_call" | custom-call | tf_op jit(solution)/shard_map/reduce_terms/pallas_call | solution.py:784
  124.5 5.8 %update.1 = (bf16[256,3584]{1,0:T(8,128)(2,1)}, bf16[256,7168]{1,0:T(8,128)(2,1)}, f32[224,1024]{1,0:T(8,128)}, bf16[224,1024]{1,0:T(8,128)(2,1)}, bf16[224,1024]{1,0:T(8,128)(2,1)}) custom-call(bf16[256,3584]{1,0:T(8,128)(2,1)} %get-tuple-element.22.dq_in, bf16[256,7168]{1,0:T(8,128)(2,1)} %get-tuple-element.23.dn_in, ...), custom_call_target="tpu_custom_call" | custom-call | tf_op jit(solution)/shard_map/update/pallas_call | solution.py:876
